TPU v7x, 512 devices: a whole 4x4x16 slice. The times are simulated.
512 devices in a mesh: row: 16 (over y, x_hi, core), col: 32 (over z, x_lo).
Axes of the slice: x: 4 (x_hi: 2, x_lo: 2; x = x_hi * 2 + x_lo), y: 4, z: 16, core: 2. Of those that a mesh axis runs over, the one named last changes fastest.
Arguments:
- ancestor_inverse: float32 [4096, 4096], P('row', 'col'), may hold values from -6 to 6
- pattern: int32 [32, 32], replicated, may hold values 0 or 1
- listed: int32 [2, 16], replicated, may hold values from 0 to 31, as said below
- panels: float32 [2, 4096, 512], P(None, ('col', 'row')), may hold values from -0.09375 to 0.09375
- parent_panels: float32 [1, 512, 512], replicated, may hold values from -0.25 to 0.25
- diag_inverse: float32 [2, 512, 512], P(None, 'row', 'col'), may hold values from -6 to 6
Outputs:
- upper_blocks: float32 [2, 4096, 512], P(None, ('col', 'row'))
- diagonal_blocks: float32 [2, 512, 512], P(None, 'row', 'col')
Inputs may be any that keep to these rules, and one draw needn't show every extreme that they name: Each row of listed names 16 different blocks.
All inputs are finite; a program needn't handle non-finite values.
Results may differ from a plain program's by a relative error of at most 0.00011.
Values sent between devices are 32-bit elements; how exact they have to be, the bound alone decides.
A program may use at most 64 MiB of HBM per device.

v0:
```python
import jax
import jax.numpy as jnp
from jax import lax
from jax.sharding import PartitionSpec as P

BLK = 128


def broadcast(value, axis, source):
    kept = jnp.where(lax.axis_index(axis) == source, value, 0).astype(value.dtype)
    return lax.psum(kept, axis)


def contract_rows(left, right):
    return lax.dot_general(
        left,
        right,
        (((0,), (0,)), ((), ())),
        precision=lax.Precision.HIGHEST,
        preferred_element_type=jnp.float32,
    )


def local(ancestor_inverse, pattern, listed, panels, parent_panels, diag_inverse):
    highest = lax.Precision.HIGHEST
    rows_here, cols_here = ancestor_inverse.shape
    row_count = lax.axis_size("row")
    col_count = lax.axis_size("col")
    column_ratio = col_count // row_count
    row_index = lax.axis_index("row")
    col_index = lax.axis_index("col")
    super_count, shard_rows, panel_width = panels.shape
    row_tiles = rows_here // BLK
    col_tiles = cols_here // BLK
    blocks = pattern.shape[0]
    tile_mask = lax.dynamic_slice(
        pattern, (row_index * row_tiles, col_index * col_tiles), (row_tiles, col_tiles)
    ).astype(jnp.float32)
    masked = (
        ancestor_inverse.reshape(row_tiles, BLK, col_tiles, BLK) * tile_mask[:, None, :, None]
    ).reshape(rows_here, cols_here)
    block_ids = jnp.arange(blocks, dtype=jnp.int32)
    listed_flags = jnp.any(listed[:, :, None] == block_ids[None, None, :], axis=1).astype(
        jnp.float32
    )
    first_row = (col_index * row_count + row_index) * shard_rows
    shard_blocks = (first_row + jnp.arange(shard_rows, dtype=jnp.int32)) // BLK
    onehot = (shard_blocks[:, None] == block_ids[None, :]).astype(jnp.float32)
    row_keep = jnp.dot(
        listed_flags, onehot.T, precision=highest, preferred_element_type=jnp.float32
    )
    kept_panels = panels * row_keep[:, :, None]
    tile_rows = panel_width // row_count
    tile_cols = panel_width // col_count
    uppers = []
    diagonals = []
    previous_upper = None
    previous_tile = None
    for supernode in range(super_count):
        column_slab = lax.all_gather(kept_panels[supernode], "row", axis=0, tiled=True)
        pieces = [
            broadcast(column_slab, "col", column_ratio * row_index + member)
            for member in range(column_ratio)
        ]
        row_slab = jnp.concatenate(pieces, axis=0)
        column_sum = lax.psum_scatter(
            contract_rows(masked, row_slab), "row", scatter_dimension=0, tiled=True
        )
        if supernode > 0:
            parent_link = parent_panels[supernode - 1]
            chained = jnp.dot(
                previous_upper, parent_link, precision=highest, preferred_element_type=jnp.float32
            )
            column_sum = column_sum + chained
        upper_part = -column_sum * row_keep[supernode][:, None]
        partial_value = -contract_rows(kept_panels[supernode], upper_part)
        if supernode > 0:
            partial_value = partial_value + contract_rows(chained, kept_panels[supernode])
            link_band = lax.dynamic_slice_in_dim(parent_link, row_index * tile_rows, tile_rows, 0)
            link_slice = lax.dynamic_slice_in_dim(parent_link, col_index * tile_cols, tile_cols, 0)
            inner = jnp.dot(
                previous_tile, link_slice, precision=highest, preferred_element_type=jnp.float32
            )
            partial_value = partial_value + contract_rows(link_band, inner)
        partial_value = lax.dynamic_update_slice(
            partial_value,
            lax.dynamic_slice(
                partial_value,
                (row_index * tile_rows, col_index * tile_cols),
                (tile_rows, tile_cols),
            )
            + diag_inverse[supernode],
            (row_index * tile_rows, col_index * tile_cols),
        )
        row_band = lax.psum_scatter(partial_value, "row", scatter_dimension=0, tiled=True)
        diag_tile = lax.psum_scatter(row_band, "col", scatter_dimension=1, tiled=True)
        previous_upper = upper_part
        previous_tile = diag_tile
        uppers.append(upper_part)
        diagonals.append(diag_tile)
    return (jnp.stack(uppers), jnp.stack(diagonals))


def solution(mesh):
    return jax.shard_map(
        local,
        mesh=mesh,
        in_specs=(
            P("row", "col"),
            P(),
            P(),
            P(None, ("col", "row"), None),
            P(),
            P(None, "row", "col"),
        ),
        out_specs=(P(None, ("col", "row"), None), P(None, "row", "col")),
        check_vma=False,
    )
```

profile of v0, /device:TPU:16, one launch (start us, length us, event | category | flops | bytes accessed | tf_op | source)
XLA Modules:
  0.0 977.3 jit_solution(14819293796184799126)
XLA Ops:
  7.2 0.0 all-reduce.3.cloned.1.call-start
  7.3 0.7 copy-done.9
  8.0 0.1 fusion.22
  8.1 0.2 fusion.26
  8.3 0.1 broadcast_multiply_fusion
  8.4 21.0 %all-gather = f32[1,128,512]{2,1,0:T(8,128)S(1)} all-gather(f32[1,8,512]{2,1,0:T(8,128)S(1)} %get-tuple-element.10), channel_id=2, replica_groups=mesh['row'=16,'col'=32] {'row'}, dimensions={1}, use_global_device_ids=true | all-gather | bytes 278528 | tf_op jit(solution)/shard_map/all_gather | solution.py:60
  29.4 23.9 %all-gather.1 = f32[1,128,512]{2,1,0:T(8,128)S(1)} all-gather(f32[1,8,512]{2,1,0:T(8,128)S(1)} %get-tuple-element.11), channel_id=3, replica_groups=mesh['row'=16,'col'=32] {'row'}, dimensions={1}, use_global_device_ids=true | all-gather | bytes 278528 | tf_op jit(solution)/shard_map/all_gather | solution.py:60
  53.3 0.9 select_bitcast_fusion.1
  54.2 0.9 select_bitcast_fusion.3
  55.1 0.0 all-reduce.3.cloned.1.call-update
  55.1 0.0 reduce-scatter.11.cloned.1.call-start
  55.1 0.9 convert_reduce_fusion
  56.0 0.1 broadcast_bitcast_fusion
  56.1 267.7 %all-reduce.3.cloned.1.call-done = (f32[128,512]{1,0:T(8,128)}, f32[128,512]{1,0:T(8,128)}, f32[128,512]{1,0:T(8,128)}, f32[128,512]{1,0:T(8,128)}) async-done(((f32[128,512]{1,0:T(8,128)}, f32[128,512]{1,0:T(8,128)}, f32[128,512]{1,0:T(8,128)}, f32[128,512]{1,0:T(8,128)}), (f32[128,512]{1,0:T(8,128)}, f32[128,512]{1,0:T(8,128)}, f32[128,512]{1,0:T(8,128)}, ...) | async-done | bytes 1048592 | tf_op jit(solution)/shard_map/psum | solution.py:11
  323.8 2.3 fusion.2
  326.1 0.0 reduce-scatter.13.cloned.1.call-start
  326.2 0.9 copy-done.2
  327.1 1.2 fusion.6
  328.3 0.0 reduce-scatter.19.cloned.1.call-start
  328.4 85.9 %reduce-scatter.11.cloned.1.call-done = f32[8,512]{1,0:T(8,128)} async-done(((f32[128,512]{1,0:T(8,128)}), f32[8,512]{1,0:T(8,128)}) %reduce-scatter.11.cloned.1.call-update) | async-done | bytes 16400 | tf_op jit(solution)/shard_map/reduce_scatter | solution.py:66
  414.3 1.8 convolution_negate_fusion.1
  416.1 0.1 bitcast_add_fusion.1
  416.2 0.7 dynamic_update_slice.6
  416.9 1.3 copy.8
  418.2 0.0 reduce-scatter.15.cloned.1.call-start
  418.3 0.6 copy-done.4
  418.9 0.6 fusion
  419.5 87.4 %reduce-scatter.13.cloned.1.call-done = f32[8,512]{1,0:T(8,128)} async-done(((f32[128,512]{1,0:T(8,128)}), f32[8,512]{1,0:T(8,128)}) %reduce-scatter.13.cloned.1.call-update) | async-done | bytes 16400 | tf_op jit(solution)/shard_map/reduce_scatter | solution.py:66
  506.9 1.8 convolution_negate_fusion
  508.7 92.5 %reduce-scatter.19.cloned.1.call-done = f32[32,512]{1,0:T(8,128)} async-done(((f32[512,512]{1,0:T(8,128)}), f32[32,512]{1,0:T(8,128)}) %reduce-scatter.19.cloned.1.call-update) | async-done | bytes 65552
  601.3 1.7 copy.9
  603.0 0.0 reduce-scatter.21.cloned.1.call-start
  603.0 1.0 convolution_add_fusion.1
  604.1 135.6 %reduce-scatter.15.cloned.1.call-done = f32[32,16]{0,1:T(8,128)} async-done(((f32[32,512]{0,1:T(8,128)}), f32[32,16]{0,1:T(8,128)}) %reduce-scatter.15.cloned.1.call-update) | async-done | bytes 2064 | tf_op jit(solution)/shard_map/reduce_scatter | solution.py:96
  739.6 0.9 fusion.16
  740.6 1.0 convolution_add_fusion
  741.6 0.1 bitcast_add_fusion
  741.7 0.7 dynamic_update_slice.7
  742.4 1.3 copy.10
  743.7 0.0 reduce-scatter.17.cloned.1.call-start
  743.8 0.6 copy-done.5
  744.4 0.1 fusion.28
  744.5 86.1 %reduce-scatter.21.cloned.1.call-done = f32[32,512]{1,0:T(8,128)} async-done(((f32[512,512]{1,0:T(8,128)}), f32[32,512]{1,0:T(8,128)}) %reduce-scatter.21.cloned.1.call-update) | async-done | bytes 65552
  830.6 1.7 copy.11
  832.3 0.1 fusion.23
  832.4 0.6 pad_maximum_fusion
  833.0 136.1 %reduce-scatter.17.cloned.1.call-done = f32[32,16]{0,1:T(8,128)} async-done(((f32[32,512]{0,1:T(8,128)}), f32[32,16]{0,1:T(8,128)}) %reduce-scatter.17.cloned.1.call-update) | async-done | bytes 2064 | tf_op jit(solution)/shard_map/reduce_scatter | solution.py:96
  969.2 1.3 pad_maximum_fusion.1
  (25 shorter events, 0.2 us)
Async XLA Ops:
  7.2 411.1 %copy-start = (f32[1,512,512]{2,1,0:T(8,128)S(1)}, f32[1,512,512]{2,1,0:T(8,128)}, u32[]{:S(2)}) copy-start(f32[1,512,512]{2,1,0:T(8,128)} %param.10) | copy-start | bytes 3145732
  7.2 316.6 %all-reduce.3.cloned.1.call-start = ((), (), s32[]{:S(2)}) async-start(), calls=%async_computation.12 | async-start | bytes 2097152 | tf_op jit(solution)/shard_map/psum | solution.py:11
  7.2 0.8 copy-start.9
  7.3 1.0 copy-start.6
  55.1 268.8 %copy-start.1 = (f32[256,128]{1,0:T(8,128)S(1)}, f32[256,128]{1,0:T(8,128)}, u32[]{:S(2)}) copy-start(f32[256,128]{1,0:T(8,128)} %param.6) | copy-start | bytes 393220
  55.1 359.2 %reduce-scatter.11.cloned.1.call-start = ((), (), s32[]{:S(2)}) async-start(), calls=%async_computation.6 | async-start | bytes 278528 | tf_op jit(solution)/shard_map/reduce_scatter | solution.py:66
  323.8 2.4 copy-start.3
  326.1 0.9 copy-start.2
  326.1 180.8 %reduce-scatter.13.cloned.1.call-start = ((), (), s32[]{:S(2)}) async-start(), calls=%async_computation.7 | async-start | bytes 278528 | tf_op jit(solution)/shard_map/reduce_scatter | solution.py:66
  328.3 273.0 %reduce-scatter.19.cloned.1.call-start = ((), (), s32[]{:S(2)}) async-start(), calls=%async_computation.10 | async-start | bytes 1114112
  414.3 1.8 copy-start.8
  418.2 0.7 copy-start.4
  418.2 321.4 %reduce-scatter.15.cloned.1.call-start = ((), (), s32[]{:S(2)}) async-start(), calls=%async_computation.8 | async-start | bytes 270336 | tf_op jit(solution)/shard_map/reduce_scatter | solution.py:96
  603.0 227.7 %reduce-scatter.21.cloned.1.call-start = ((), (), s32[]{:S(2)}) async-start(), calls=%async_computation.11 | async-start | bytes 1114112
  743.7 0.7 copy-start.5
  743.7 225.4 %reduce-scatter.17.cloned.1.call-start = ((), (), s32[]{:S(2)}) async-start(), calls=%async_computation.9 | async-start | bytes 270336 | tf_op jit(solution)/shard_map/reduce_scatter | solution.py:96
  832.4 136.7 %copy-start.7 = (f32[32,16]{0,1:T(8,128)S(1)}, f32[32,16]{0,1:T(8,128)}, u32[]{:S(2)}) copy-start(f32[32,16]{0,1:T(8,128)} %reduce-scatter.15.cloned.1.call-done) | copy-start | bytes 6148
Sparse Core Ops, SparseCore 0:
  55.2 268.5 all-reduce.2
  329.0 85.2 reduce-scatter.10
  419.5 87.3 reduce-scatter.12
  512.1 89.1 reduce-scatter.18
  603.9 135.6 reduce-scatter.14
  744.8 85.7 reduce-scatter.20
  833.4 135.6 reduce-scatter.16
where the time goes:
time: 978 us; the launch traced here: 977 us
  waiting for transfers between devices  892 us (91%)
  blocking collectives  44.9 us (5%)
  between operations  14.3 us (1%)
  matrix products  10.9 us (1%)
  local copies, waits for them, and re-layouts  10.3 us (1%)
    reduce_scatter x2, waiting for transfers between devices, local(): lax.psum_scatter(row_band, 'col', scatter_dimension=1, tiled=True)  272 us
    psum x1, waiting for transfers between devices, broadcast(): return lax.psum(kept, axis)  268 us
    unnamed x9, waiting for transfers between devices  179 us
    reduce_scatter x2, waiting for transfers between devices, local(): lax.psum_scatter(contract_rows(masked, row_slab), 'row', scatter_dimensio...  173 us
    all_gather x2, blocking collectives, local(): lax.all_gather(kept_panels[supernode], 'row', axis=0, tiled=True)  44.9 us
  transfers between devices with their start and end apart: 7, of which 7 were waited for; matrix products, arithmetic and copies ran while one was open for 1% of the time, Pallas kernels for 0%

commit v1 on v0

v1 whole, which is shorter than its diff:
```python
import functools

import jax
import jax.numpy as jnp
from jax import lax
from jax.experimental import pallas as pl
from jax.experimental.pallas import tpu as pltpu
from jax.sharding import PartitionSpec as P

BLK = 128
LANES = 128
MESH = pl.DeviceIdType.MESH
F32 = jnp.float32


def dot(left, right):
    return jnp.dot(left, right, precision=lax.Precision.HIGHEST, preferred_element_type=F32)


def dot_rows(left, right):
    return lax.dot_general(
        left,
        right,
        (((0,), (0,)), ((), ())),
        precision=lax.Precision.HIGHEST,
        preferred_element_type=F32,
    )


def exchange(parts, width):
    parts = list(parts)
    count = len(parts)
    segment = lax.broadcasted_iota(jnp.int32, parts[0].shape, 1) // width
    bit = count // 2
    while bit:
        low = (segment % (2 * bit)) < bit
        for a in range(count):
            if a & bit == 0:
                first, second = parts[a], parts[a + bit]
                parts[a] = jnp.where(low, first, pltpu.roll(second, bit * width, 1))
                parts[a + bit] = jnp.where(low, pltpu.roll(first, LANES - bit * width, 1), second)
        bit //= 2
    return parts


def kernel(
    rows,
    cols,
    a_ref,
    pattern_ref,
    listed_ref,
    panel_ref,
    link_ref,
    diag_ref,
    upper_ref,
    out_ref,
    panels,
    anc,
    slab,
    partial,
    shares,
    left_out,
    left_in,
    kept_out,
    kept_in,
    upper_in,
    sum_out,
    sum_in,
    band,
    tile_out,
    tile_in,
    anc_send,
    anc_recv,
    ring_send,
    ring_recv,
    sems,
):
    row, col = lax.axis_index("row"), lax.axis_index("col")
    depth = cols // 2
    z, side = lax.div(col, 2), lax.rem(col, 2)
    pair, core = lax.div(row, 2), lax.rem(row, 2)
    height = panel_ref.shape[1]
    width = panel_ref.shape[2]
    half = width // 2
    plane = 2 * rows
    me = side * rows + row
    tall = a_ref.shape[0]
    band_rows = width // rows
    band_cols = width // cols

    def place(index):
        return (lax.rem(index, rows), 2 * z + lax.div(index, rows))

    def peer(step):
        return lax.rem(me + step, plane)

    with jax.named_scope("greet"):
        barrier = pltpu.get_barrier_semaphore()

        @pl.loop(1, plane)
        def _(step):
            pl.semaphore_signal(barrier, inc=1, device_id=place(peer(step)), device_id_type=MESH)

        @pl.loop(2, cols)
        def _(step):
            other = lax.rem(2 * z + step, cols)
            pl.semaphore_signal(barrier, inc=1, device_id=(row, other), device_id_type=MESH)

        def keep(s):
            found = listed_ref[s, 0] == col
            for i in range(1, listed_ref.shape[1]):
                found = jnp.logical_or(found, listed_ref[s, i] == col)
            return jnp.where(found, 1.0, 0.0).astype(F32)

        flag0, flag1 = keep(0), keep(1)
        kept0 = panel_ref[0] * flag0
        kept1 = panel_ref[1] * flag1
        panels[z, 0] = kept0
        panels[z, 1] = kept1
        for i in range(tall // BLK):
            present = pattern_ref[(tall // BLK) * row + i, col].astype(F32)
            anc[side, pl.ds(core * tall + i * BLK, BLK), :] = a_ref[pl.ds(i * BLK, BLK), :] * present
        pl.semaphore_wait(barrier, plane - 1 + cols - 2)

    def ring(step, right, part=slice(None)):
        sign = -1 if right else 1
        block = lax.rem(z + depth + sign * step, depth)
        target = lax.rem(col + (2 if right else cols - 2), cols)
        piece = panels.at[block] if isinstance(part, slice) else panels.at[block, part]
        way = 0 if right else 1
        return pltpu.make_async_remote_copy(
            src_ref=piece,
            dst_ref=piece,
            send_sem=ring_send.at[way, step],
            recv_sem=ring_recv.at[way, step],
            device_id=(row, target),
            device_id_type=MESH,
        )

    slab_sent, slab_got, left_sent, left_got, kept_sent, kept_got = (sems.at[i] for i in range(6))
    share_sent, share_got, upper_sent, upper_got, sum_sent, sum_got = (sems.at[i] for i in range(6, 12))
    tile_sent, tile_got = sems.at[12], sems.at[13]

    def spread(offset):
        block = lax.rem(z + depth + offset, depth)
        owner = lax.div(block, 2)
        slot = (lax.rem(block, 2) * 2 + side) * rows + row
        for step in range(4):
            quarter = lax.rem(2 * core + side + step, 4)
            super_of, half_of = lax.div(quarter, 2), lax.rem(quarter, 2)
            source = panels.at[block, super_of, :, pl.ds(pl.multiple_of(half_of * half, LANES), half)]

            def send():
                pltpu.make_async_remote_copy(
                    src_ref=source,
                    dst_ref=slab.at[slot],
                    send_sem=slab_sent,
                    recv_sem=slab_got,
                    device_id=(2 * owner + super_of, 2 * z + half_of),
                    device_id_type=MESH,
                ).start()

            if step == 0:
                pl.when(owner != pair)(send)

                @pl.when(owner == pair)
                def _():
                    pltpu.make_async_copy(source, slab.at[slot], slab_got).start()
            else:
                send()

    def anc_copy(i):
        other_row = 2 * pair + (core + i) % 2
        other_col = 2 * z + (side + i // 2) % 2
        piece = anc.at[side, pl.ds(core * tall, tall), :]
        return pltpu.make_async_remote_copy(
            src_ref=piece,
            dst_ref=piece,
            send_sem=anc_send.at[i - 1],
            recv_sem=anc_recv.at[i - 1],
            device_id=(other_row, other_col),
            device_id_type=MESH,
        )

    steps = depth // 2
    with jax.named_scope("start"):
        ring(0, True).start()
        ring(0, False).start()
        for i in (1, 2, 3):
            anc_copy(i).start()
        spread(0)

    with jax.named_scope("early"):
        chained_kept = dot(kept0, link_ref[...])
        mixed = kept1 - chained_kept
        tile = diag_ref[0]
        link_band = link_ref[pl.ds(pl.multiple_of(row * band_rows, 8), band_rows), :]
        extra = dot_rows(tile, link_band)
        per = LANES // band_rows
        for g in range(width // LANES):
            cut = slice(g * LANES, (g + 1) * LANES)
            packed = exchange([kept0[:, cut], kept1[:, cut], mixed[:, cut], extra[:height, cut]], band_rows)
            for j in range(per):
                left_out[g * per + j, :, :LANES] = packed[j]
                tail = extra[height:, cut]
                if j:
                    tail = pltpu.roll(tail, LANES - j * band_rows, 1)
                left_out[g * per + j, :, LANES:] = tail
        for h in range(2):
            kept_out[h] = kept1[:, h * half : (h + 1) * half]
        left_in[me] = left_out[row]
        kept_in[me] = kept_out[side]

        @pl.loop(1, plane)
        def _(step):
            other = peer(step)
            target = place(other)
            pltpu.make_async_remote_copy(
                src_ref=left_out.at[target[0]],
                dst_ref=left_in.at[me],
                send_sem=left_sent,
                recv_sem=left_got,
                device_id=target,
                device_id_type=MESH,
            ).start()
            pltpu.make_async_remote_copy(
                src_ref=kept_out.at[lax.div(other, rows)],
                dst_ref=kept_in.at[me],
                send_sem=kept_sent,
                recv_sem=kept_got,
                device_id=target,
                device_id_type=MESH,
            ).start()

    with jax.named_scope("ring"):

        @pl.loop(0, steps - 1)
        def _(step):
            ring(step, True).wait_recv()
            ring(step, False).wait_recv()

            @pl.when(step < steps - 2)
            def _():
                ring(step + 1, True).start()
                ring(step + 1, False).start()

            @pl.when(step == steps - 2)
            def _():
                ring(steps - 1, True, 0).start()
                ring(steps - 1, False, 1).start()

            spread(-step - 1)
            spread(step + 1)

        ring(steps - 1, True, 0).wait_recv()
        ring(steps - 1, False, 1).wait_recv()
        spread(steps)

    def wait_for(ref, sem):
        pltpu.make_async_copy(ref, ref, sem).wait()

    with jax.named_scope("slab"):
        for i in (1, 2, 3):
            anc_copy(i).wait_recv()
        wait_for(slab, slab_got)
    with jax.named_scope("product"):
        kept_rows = slab[...].reshape(2 * tall, half)
        for i in range(2):
            part = dot_rows(anc[i], kept_rows)
            partial[pl.ds(i * rows, rows)] = part.reshape(rows, height, half)

    slot = (2 * core + side) * (rows // 2) + pair
    with jax.named_scope("scatter"):
        shares[slot] = partial[me]

        @pl.loop(1, plane)
        def _(step):
            other = peer(step)
            pltpu.make_async_remote_copy(
                src_ref=partial.at[other],
                dst_ref=shares.at[slot],
                send_sem=share_sent,
                recv_sem=share_got,
                device_id=place(other),
                device_id_type=MESH,
            ).start()

    with jax.named_scope("linkterm"):
        wait_for(left_in.at[pl.ds(0, plane - 1)], left_got)
        wait_for(kept_in.at[pl.ds(0, plane - 1)], kept_got)
        lefts = left_in[...].reshape(plane * height, 2 * LANES)
        kept_half = kept_in[...].reshape(plane * height, half)
        column_half = pl.ds(pl.multiple_of(side * half, LANES), half)
        link_half = link_ref[:, column_half]
        group = pl.ds(pl.multiple_of(lax.div(row, per) * LANES, LANES), LANES)
        link_group = link_ref[:, group]
        link_rows = link_ref[pl.ds(pl.multiple_of(z * 2 * band_cols, 8), 2 * band_cols), column_half]

        def repeat(i):
            return jnp.concatenate(
                [link_rows[s * band_cols + i : s * band_cols + i + height] for s in range(2) for _ in range(rows)],
                axis=0,
            )

        constant = (
            dot_rows(lefts[:, :LANES], repeat(0))[3 * band_rows :]
            + dot_rows(lefts[:, LANES:], repeat(height))[:band_rows]
        )

    with jax.named_scope("shares"):
        wait_for(shares.at[pl.ds(0, plane - 1)], share_got)
        quarters = []
        for q in range(4):
            total = shares[q * (rows // 2)]
            for i in range(1, rows // 2):
                total = total + shares[q * (rows // 2) + i]
            quarters.append(total)
        sum0 = jnp.concatenate(quarters[:2], axis=1)
        sum1 = jnp.concatenate(quarters[2:], axis=1)
        upper0 = -sum0 * flag0
        upper_in[me] = upper0
        sum_out[0] = quarters[2]
        sum_out[1] = quarters[3]
        sum_in[me] = sum_out[side]

    with jax.named_scope("gather"):

        @pl.loop(1, plane)
        def _(step):
            other = peer(step)
            target = place(other)
            pltpu.make_async_remote_copy(
                src_ref=upper_in.at[me],
                dst_ref=upper_in.at[me],
                send_sem=upper_sent,
                recv_sem=upper_got,
                device_id=target,
                device_id_type=MESH,
            ).start()
            pltpu.make_async_remote_copy(
                src_ref=sum_out.at[lax.div(other, rows)],
                dst_ref=sum_in.at[me],
                send_sem=sum_sent,
                recv_sem=sum_got,
                device_id=target,
                device_id_type=MESH,
            ).start()

        upper_ref[0] = upper0
        upper_ref[1] = -(sum1 + dot(upper0, link_ref[...])) * flag1
        wait_for(upper_in.at[pl.ds(0, plane - 1)], upper_got)
        wait_for(sum_in.at[pl.ds(0, plane - 1)], sum_got)

    with jax.named_scope("diagonal"):
        uppers = upper_in[...].reshape(plane * height, width)
        sums = sum_in[...].reshape(plane * height, half)
        chained_half = dot(uppers, link_half)
        chained_group = dot(uppers, link_group)
        band[...] = dot_rows(chained_group, kept_half)
        crossed = band[pl.ds(pl.multiple_of(lax.rem(row, per) * band_rows, 8), band_rows), :]
        upper_half = upper_in[:, :, column_half].reshape(plane * height, half)
        first = lefts[:, :LANES]
        tile0 = -dot_rows(first, upper_half)[:band_rows]
        tile1 = (
            dot_rows(first, sums)[band_rows : 2 * band_rows]
            + dot_rows(first, chained_half)[2 * band_rows : 3 * band_rows]
            + crossed
            + constant
        )
        share = LANES // band_cols
        for g in range(half // LANES):
            cut = slice(g * LANES, (g + 1) * LANES)
            pieces = [t[8 * i : 8 * i + 8, cut] for t in (tile0, tile1) for i in range(band_rows // 8)]
            for j, packed in enumerate(exchange(pieces, band_cols)):
                tile_out[g * share + j] = packed

    count = cols // 2
    own = lax.div(col, count) == side
    with jax.named_scope("tiles"):

        @pl.loop(0, count)
        def _(step):
            other = lax.rem(col + step, count)
            target = side * count + other

            @pl.when(target != col)
            def _():
                pltpu.make_async_remote_copy(
                    src_ref=tile_out.at[other],
                    dst_ref=tile_in.at[z],
                    send_sem=tile_sent,
                    recv_sem=tile_got,
                    device_id=(row, target),
                    device_id_type=MESH,
                ).start()

            @pl.when(target == col)
            def _():
                pltpu.make_async_copy(tile_out.at[other], tile_in.at[z], tile_got).start()

        wait_for(tile_in, tile_got)
        total = tile_in[0]
        for i in range(1, count):
            total = total + tile_in[i]
        for s in range(2):
            for i in range(band_rows // 8):
                at = (s * (band_rows // 8) + i) * band_cols
                out_ref[s, 8 * i : 8 * i + 8, :] = (
                    diag_ref[s, 8 * i : 8 * i + 8, :] + total[:, at : at + band_cols]
                )

    with jax.named_scope("drain"):
        for i in (1, 2, 3):
            anc_copy(i).wait_send()

        @pl.loop(0, steps - 1)
        def _(step):
            ring(step, True).wait_send()
            ring(step, False).wait_send()

        ring(steps - 1, True, 0).wait_send()
        ring(steps - 1, False, 1).wait_send()
        wait_for(slab.at[pl.ds(0, 4 * rows - 2)], slab_sent)
        wait_for(left_in.at[pl.ds(0, plane - 1)], left_sent)
        wait_for(kept_in.at[pl.ds(0, plane - 1)], kept_sent)
        wait_for(shares.at[pl.ds(0, plane - 1)], share_sent)
        wait_for(upper_in.at[pl.ds(0, plane - 1)], upper_sent)
        wait_for(sum_in.at[pl.ds(0, plane - 1)], sum_sent)

        @pl.when(own)
        def _():
            wait_for(tile_in.at[pl.ds(0, count - 1)], tile_sent)

        @pl.when(jnp.logical_not(own))
        def _():
            wait_for(tile_in, tile_sent)


def local(rows, cols, ancestor_inverse, pattern, listed, panels, parent_panels, diag_inverse):
    supers, height, width = panels.shape
    tall, wide = ancestor_inverse.shape
    depth = cols // 2
    plane = 2 * rows
    half = width // 2
    count = cols // 2
    vmem = pl.BlockSpec(memory_space=pltpu.VMEM)
    smem = pl.BlockSpec(memory_space=pltpu.SMEM)
    return pl.pallas_call(
        functools.partial(kernel, rows, cols),
        out_shape=(
            jax.ShapeDtypeStruct(panels.shape, F32),
            jax.ShapeDtypeStruct(diag_inverse.shape, F32),
        ),
        in_specs=[vmem, smem, smem, vmem, vmem, vmem],
        out_specs=(vmem, vmem),
        scratch_shapes=[
            pltpu.VMEM((depth, supers, height, width), F32),
            pltpu.VMEM((2, 2 * tall, wide), F32),
            pltpu.VMEM((4 * rows, height, half), F32),
            pltpu.VMEM((plane, height, half), F32),
            pltpu.VMEM((plane, height, half), F32),
            pltpu.VMEM((rows, height, 2 * LANES), F32),
            pltpu.VMEM((plane, height, 2 * LANES), F32),
            pltpu.VMEM((2, height, half), F32),
            pltpu.VMEM((plane, height, half), F32),
            pltpu.VMEM((plane, height, width), F32),
            pltpu.VMEM((2, height, half), F32),
            pltpu.VMEM((plane, height, half), F32),
            pltpu.VMEM((LANES, half), F32),
            pltpu.VMEM((count, 8, LANES), F32),
            pltpu.VMEM((count, 8, LANES), F32),
            pltpu.SemaphoreType.DMA((3,)),
            pltpu.SemaphoreType.DMA((3,)),
            pltpu.SemaphoreType.DMA((2, depth // 2)),
            pltpu.SemaphoreType.DMA((2, depth // 2)),
            pltpu.SemaphoreType.DMA((14,)),
        ],
        compiler_params=pltpu.CompilerParams(
            collective_id=0, has_side_effects=True, vmem_limit_bytes=48 * 1024 * 1024
        ),
    )(ancestor_inverse, pattern, listed, panels, parent_panels[0], diag_inverse)


def solution(mesh):
    rows, cols = mesh.shape["row"], mesh.shape["col"]
    return jax.shard_map(
        functools.partial(local, rows, cols),
        mesh=mesh,
        in_specs=(
            P("row", "col"),
            P(),
            P(),
            P(None, ("col", "row"), None),
            P(),
            P(None, "row", "col"),
        ),
        out_specs=(P(None, ("col", "row"), None), P(None, "row", "col")),
        check_vma=False,
    )
```

time: 978 us -> 85.3 us (0.09)
  the two profiles are of different devices: /device:TPU:16 before, /device:TPU:1 now
where the time goes in v1:
time: 85.3 us; the launch traced here: 83.6 us
  Pallas kernels  78.7 us (92%)
  local copies, waits for them, and re-layouts  4.24 us (5%)
    pallas_call x1, Pallas kernels, local(): pl.pallas_call(functools.partial(kernel, rows, cols), out_shape=(jax.Shap...  78.7 us
    unnamed x12, local copies, waits for them, and re-layouts  3.56 us

profile of v1, /device:TPU:1, one launch (start us, length us, event | category | flops | bytes accessed | tf_op | source)
XLA Modules:
  0.0 83.6 jit_solution(6469864421808391229)
XLA Ops:
  0.6 0.0 copy-start.2
  0.6 0.0 copy-start.3
  0.7 0.0 copy-start.4
  0.7 0.8 copy.8.diag_ref
  1.5 0.0 copy-done.2
  1.5 0.0 copy-done.3
  1.5 0.0 copy-done.4
  1.5 0.0 copy-start
  1.5 1.2 %copy-done = f32[1,512,512]{2,1,0:T(8,128)S(1)} copy-done((f32[1,512,512]{2,1,0:T(8,128)S(1)}, f32[1,512,512]{2,1,0:T(8,128)}, u32[]{:S(2)}) %copy-start) | copy-done | bytes 1048600
  2.7 0.0 copy-start.1
  2.7 0.9 %copy-done.1 = f32[256,128]{1,0:T(8,128)S(1)} copy-done((f32[256,128]{1,0:T(8,128)S(1)}, f32[256,128]{1,0:T(8,128)}, u32[]{:S(2)}) %copy-start.1) | copy-done | bytes 131096
  3.6 78.7 %shard_map.77 = (f32[2,8,512]{2,1,0:T(8,128)S(1)}, f32[2,32,16]{2,1,0:T(8,128)S(1)}) custom-call(f32[256,128]{1,0:T(8,128)S(1)} %copy-done.1, s32[32,32]{1,0:T(8,128)S(1)} %copy-done.3, s32[2,16]{1,0:T(2,128)S(1)} %copy-done.4, f32[2,8,512]{2,1,0:T(8,128)S(1)} %copy-done.2, f32[512,512]{1,0:T(8,128)S(1)} %bitcast.1, f32[2,32,16]{2,1,0:T(8,128)S(1)} %copy.8.diag_ref), custom_call_target="tpu_custom_call" | custom-call | tf_op jit(solution)/shard_map/pallas_call | solution.py:448
  82.3 0.7 copy.9
  83.0 0.6 copy.11
Async XLA Ops:
  0.6 0.8 %copy-start.2 = (f32[2,8,512]{2,1,0:T(8,128)S(1)}, f32[2,8,512]{2,1,0:T(8,128)}, u32[]{:S(2)}) copy-start(f32[2,8,512]{2,1,0:T(8,128)} %panel_ref.1) | copy-start | bytes 98308
  0.6 0.8 copy-start.3
  0.7 0.8 copy-start.4
  1.5 1.2 %copy-start = (f32[1,512,512]{2,1,0:T(8,128)S(1)}, f32[1,512,512]{2,1,0:T(8,128)}, u32[]{:S(2)}) copy-start(f32[1,512,512]{2,1,0:T(8,128)} %param.10) | copy-start | bytes 3145732
  2.7 0.9 %copy-start.1 = (f32[256,128]{1,0:T(8,128)S(1)}, f32[256,128]{1,0:T(8,128)}, u32[]{:S(2)}) copy-start(f32[256,128]{1,0:T(8,128)} %a_ref.1) | copy-start | bytes 393220

commit v2 on v1

v2 whole, which is shorter than its diff:
```python
import functools

import jax
import jax.numpy as jnp
from jax import lax
from jax.experimental import pallas as pl
from jax.experimental.pallas import tpu as pltpu
from jax.sharding import PartitionSpec as P

BLK = 128
LANES = 128
MESH = pl.DeviceIdType.MESH
F32 = jnp.float32


def dot(left, right):
    return jnp.dot(left, right, precision=lax.Precision.HIGHEST, preferred_element_type=F32)


def dot_rows(left, right):
    return lax.dot_general(
        left,
        right,
        (((0,), (0,)), ((), ())),
        precision=lax.Precision.HIGHEST,
        preferred_element_type=F32,
    )


def exchange(parts, width):
    parts = list(parts)
    count = len(parts)
    segment = lax.broadcasted_iota(jnp.int32, parts[0].shape, 1) // width
    bit = count // 2
    while bit:
        low = (segment % (2 * bit)) < bit
        for a in range(count):
            if a & bit == 0:
                first, second = parts[a], parts[a + bit]
                parts[a] = jnp.where(low, first, pltpu.roll(second, bit * width, 1))
                parts[a + bit] = jnp.where(low, pltpu.roll(first, LANES - bit * width, 1), second)
        bit //= 2
    return parts


def kernel(
    rows,
    cols,
    a_hbm,
    pattern_ref,
    listed_ref,
    panel_hbm,
    link_hbm,
    diag_hbm,
    upper_ref,
    out_ref,
    a_ref,
    panel_ref,
    link_ref,
    diag_ref,
    panels,
    anc,
    slab,
    partial,
    shares,
    left_out,
    left_in,
    kept_out,
    kept_in,
    gather_out,
    gather_in,
    tile_out,
    tile_in,
    load_sems,
    anc_send,
    anc_recv,
    far_send,
    far_recv,
    sems,
):
    row, col = lax.axis_index("row"), lax.axis_index("col")
    depth = cols // 2
    z, side = lax.div(col, 2), lax.rem(col, 2)
    pair, core = lax.div(row, 2), lax.rem(row, 2)
    pairs = rows // 2
    height = panel_ref.shape[1]
    width = panel_ref.shape[2]
    half = width // 2
    plane = 2 * rows
    me = side * rows + row
    slot_me = (core * 2 + side) * pairs + pair
    tall = a_ref.shape[0]
    band_rows = width // rows
    band_cols = width // cols
    count = cols // 2
    own = lax.div(col, count) == side
    own_slab = lax.rem(lax.div(z, 2), 2) == lax.rem(pair, 2)

    (slab_sent, slab_got, left_sent, left_got, kept_sent, kept_got, share_sent, share_got) = (
        sems.at[i] for i in range(8)
    )
    gather_sent, gather_got, pass_sent, pass_got, tile_sent, tile_got = (sems.at[i] for i in range(8, 14))

    def wait_for(ref, sem):
        pltpu.make_async_copy(ref, ref, sem).wait()

    def place(index):
        return (lax.rem(index, rows), 2 * z + lax.div(index, rows))

    def peer(step):
        return lax.rem(me + step, plane)

    def plane_at(offset):
        return lax.rem(z + depth + offset, depth)

    def near(residue, core_from):
        gap = lax.rem(residue, 4)
        return jnp.where(gap == 3, -1, jnp.where(gap == 2, 2 - 4 * core_from, gap))

    loads = [
        pltpu.make_async_copy(panel_hbm, panel_ref, load_sems.at[0]),
        pltpu.make_async_copy(a_hbm, a_ref, load_sems.at[1]),
        pltpu.make_async_copy(diag_hbm, diag_ref, load_sems.at[2]),
        pltpu.make_async_copy(link_hbm, link_ref, load_sems.at[3]),
    ]
    with jax.named_scope("greet"):
        for load in loads:
            load.start()
        barrier = pltpu.get_barrier_semaphore()

        def greet(device):
            pl.semaphore_signal(barrier, inc=1, device_id=device, device_id_type=MESH)

        for far in (2, 1, 3):
            greet((row, lax.rem(col + 8 * far, cols)))

        @pl.loop(0, depth)
        def _(step):
            source = 2 * plane_at(step) + lax.div(col, count)

            @pl.when(source != col)
            def _():
                greet((row, source))

        @pl.loop(0, plane)
        def _(step):
            other = peer(step)
            row_from, side_from = lax.rem(other, rows), lax.div(other, rows)

            @pl.when(step > 0)
            def _():
                greet(place(other))

            for i in range(2):
                offset = near(z + depth - lax.rem(2 * pair + i, 4), lax.rem(row_from, 2))

                @pl.when(jnp.logical_or(step > 0, offset != 0))
                def _():
                    greet((row_from, 2 * plane_at(-offset) + side_from))

        def keep(s):
            found = listed_ref[s, 0] == col
            for i in range(1, listed_ref.shape[1]):
                found = jnp.logical_or(found, listed_ref[s, i] == col)
            return jnp.where(found, 1.0, 0.0).astype(F32)

        flag0, flag1 = keep(0), keep(1)
        loads[0].wait()
        kept0 = panel_ref[0] * flag0
        kept1 = panel_ref[1] * flag1
        panels[lax.div(z, 4), 0] = kept0
        panels[lax.div(z, 4), 1] = kept1
        loads[1].wait()
        for i in range(tall // BLK):
            present = pattern_ref[(tall // BLK) * row + i, col].astype(F32)
            anc[side, pl.ds(core * tall + i * BLK, BLK), :] = a_ref[pl.ds(i * BLK, BLK), :] * present
        slab_targets = 4 * rows - own_slab.astype(jnp.int32)
        tile_targets = count - own.astype(jnp.int32)
        pl.semaphore_wait(barrier, plane - 1 + 3 + slab_targets + tile_targets)

    def far_copy(j):
        piece = panels.at[lax.div(z, 4)]
        return pltpu.make_async_remote_copy(
            src_ref=piece,
            dst_ref=piece,
            send_sem=far_send.at[j - 1],
            recv_sem=far_recv.at[j - 1],
            device_id=(row, lax.rem(col + 8 * j, cols)),
            device_id_type=MESH,
        )

    def spread(j):
        block = plane_at(-4 * j)
        owner = lax.div(block, 2)
        slot = (lax.rem(block, 2) * 2 + side) * rows + row
        for offset in (2 - 4 * core, 1, -1, 0):
            for step in range(4):
                quarter = lax.rem(2 * core + side + step, 4)
                super_of, half_of = lax.div(quarter, 2), lax.rem(quarter, 2)
                source = panels.at[
                    lax.div(block, 4), super_of, :, pl.ds(pl.multiple_of(half_of * half, LANES), half)
                ]

                def send():
                    pltpu.make_async_remote_copy(
                        src_ref=source,
                        dst_ref=slab.at[slot],
                        send_sem=slab_sent,
                        recv_sem=slab_got,
                        device_id=(2 * owner + super_of, 2 * plane_at(offset) + half_of),
                        device_id_type=MESH,
                    ).start()

                if step == 0 and isinstance(offset, int) and offset == 0:
                    pl.when(owner != pair)(send)

                    @pl.when(owner == pair)
                    def _():
                        pltpu.make_async_copy(source, slab.at[slot], slab_got).start()
                else:
                    send()

    def anc_copy(i):
        other_row = 2 * pair + (core + i) % 2
        other_col = 2 * z + (side + i // 2) % 2
        piece = anc.at[side, pl.ds(core * tall, tall), :]
        return pltpu.make_async_remote_copy(
            src_ref=piece,
            dst_ref=piece,
            send_sem=anc_send.at[i - 1],
            recv_sem=anc_recv.at[i - 1],
            device_id=(other_row, other_col),
            device_id_type=MESH,
        )

    with jax.named_scope("start"):
        for j in (2, 1, 3):
            far_copy(j).start()
        for i in (1, 2, 3):
            anc_copy(i).start()
        spread(0)

    with jax.named_scope("early"):
        loads[2].wait()
        loads[3].wait()
        mixed = kept1 - dot(kept0, link_ref[...])
        link_band = link_ref[pl.ds(pl.multiple_of(row * band_rows, 8), band_rows), :]
        extra = dot(diag_ref[0], link_band)
        per = LANES // band_rows
        for g in range(width // LANES):
            cut = slice(g * LANES, (g + 1) * LANES)
            packed = exchange([kept0[:, cut], kept1[:, cut], mixed[:, cut], extra[:height, cut]], band_rows)
            for j in range(per):
                left_out[g * per + j, :, :LANES] = packed[j]
                tail = extra[height:, cut]
                if j:
                    tail = pltpu.roll(tail, LANES - j * band_rows, 1)
                left_out[g * per + j, :, LANES:] = tail
        for h in range(2):
            kept_out[h] = kept1[:, h * half : (h + 1) * half]
        left_in[slot_me] = left_out[row]
        kept_in[slot_me] = kept_out[side]

        @pl.loop(1, plane)
        def _(step):
            other = peer(step)
            target = place(other)
            pltpu.make_async_remote_copy(
                src_ref=left_out.at[target[0]],
                dst_ref=left_in.at[slot_me],
                send_sem=left_sent,
                recv_sem=left_got,
                device_id=target,
                device_id_type=MESH,
            ).start()
            pltpu.make_async_remote_copy(
                src_ref=kept_out.at[lax.div(other, rows)],
                dst_ref=kept_in.at[slot_me],
                send_sem=kept_sent,
                recv_sem=kept_got,
                device_id=target,
                device_id_type=MESH,
            ).start()

    with jax.named_scope("spread"):
        for j in (1, 3, 2):
            far_copy(j).wait_recv()
            spread(j)

    with jax.named_scope("slab"):
        for i in (1, 2, 3):
            anc_copy(i).wait_recv()
        wait_for(slab, slab_got)
    with jax.named_scope("product"):
        kept_rows = slab[...].reshape(2 * tall, half)
        for i in range(2):
            part = dot_rows(anc[i], kept_rows)
            partial[pl.ds(i * rows, rows)] = part.reshape(rows, height, half)

    slot = (2 * core + side) * pairs + pair
    with jax.named_scope("scatter"):
        shares[slot] = partial[me]

        @pl.loop(1, plane)
        def _(step):
            other = peer(step)
            pltpu.make_async_remote_copy(
                src_ref=partial.at[other],
                dst_ref=shares.at[slot],
                send_sem=share_sent,
                recv_sem=share_got,
                device_id=place(other),
                device_id_type=MESH,
            ).start()

    with jax.named_scope("linkterm"):
        wait_for(left_in.at[pl.ds(0, plane - 1)], left_got)
        wait_for(kept_in.at[pl.ds(0, plane - 1)], kept_got)
        lefts = left_in[...].reshape(plane * height, 2 * LANES)
        kept_half = kept_in[...].reshape(plane * height, half)
        column_half = pl.ds(pl.multiple_of(side * half, LANES), half)
        link_half = link_ref[:, column_half]
        group = pl.ds(pl.multiple_of(lax.div(row, per) * LANES, LANES), LANES)
        link_group = link_ref[:, group]
        link_rows = link_ref[pl.ds(pl.multiple_of(z * 2 * band_cols, 8), 2 * band_cols), column_half]

        def repeat(i):
            return jnp.concatenate(
                [
                    link_rows[s * band_cols + i : s * band_cols + i + height]
                    for _ in range(2)
                    for s in range(2)
                    for _ in range(pairs)
                ],
                axis=0,
            )

        constant = pltpu.roll(dot_rows(repeat(0), lefts[:, :LANES]), 2 * band_rows, 1) + pltpu.roll(
            dot_rows(repeat(height), lefts[:, LANES:]), band_rows, 1
        )

    with jax.named_scope("shares"):
        wait_for(shares.at[pl.ds(0, plane - 1)], share_got)
        quarters = []
        for q in range(4):
            total = shares[q * pairs]
            for i in range(1, pairs):
                total = total + shares[q * pairs + i]
            quarters.append(total)
        sum0 = jnp.concatenate(quarters[:2], axis=1)
        sum1 = jnp.concatenate(quarters[2:], axis=1)
        upper0 = -sum0 * flag0
        for h in range(2):
            gather_out[h, :, :width] = upper0
            gather_out[h, :, width:] = quarters[2 + h]
        gather_in[slot_me] = gather_out[side]

    with jax.named_scope("gather"):
        chip = side * pairs + pair

        @pl.loop(1, rows)
        def _(step):
            other = lax.rem(chip + step, rows)
            pltpu.make_async_remote_copy(
                src_ref=gather_out.at[lax.div(other, pairs)],
                dst_ref=gather_in.at[slot_me],
                send_sem=gather_sent,
                recv_sem=gather_got,
                device_id=(2 * lax.rem(other, pairs) + core, 2 * z + lax.div(other, pairs)),
                device_id_type=MESH,
            ).start()

        upper_ref[0] = upper0
        upper_ref[1] = -(sum1 + dot(upper0, link_ref[...])) * flag1
        wait_for(gather_in.at[pl.ds(0, rows - 1)], gather_got)
        mine = gather_in.at[pl.ds(core * rows, rows)]
        swap = pltpu.make_async_remote_copy(
            src_ref=mine,
            dst_ref=mine,
            send_sem=pass_sent,
            recv_sem=pass_got,
            device_id=(2 * pair + 1 - core, col),
            device_id_type=MESH,
        )
        swap.start()
        swap.wait_recv()

    with jax.named_scope("diagonal"):
        uppers = gather_in[:, :, :width].reshape(plane * height, width)
        sums = gather_in[:, :, width:].reshape(plane * height, half)
        chained_half = dot(uppers, link_half)
        chained_group = dot(uppers, link_group)
        upper_half = gather_in[:, :, column_half].reshape(plane * height, half)
        first = lefts[:, :LANES]
        turn = lax.rem(LANES + band_rows - lax.rem(row, per) * band_rows, LANES)
        later = (
            dot_rows(sums, first)
            + pltpu.roll(dot_rows(chained_half, first), LANES - band_rows, 1)
            + pltpu.roll(dot_rows(kept_half, chained_group), turn, 1)
            + constant
        )
        lane = lax.broadcasted_iota(jnp.int32, (half, LANES), 1)
        tiles = jnp.where(lane < band_rows, -dot_rows(upper_half, first), later)
        low = lane[:8] < 2 * band_rows
        for j in range(count):
            top = tiles[band_cols * j : band_cols * j + 8]
            bottom = tiles[band_cols * j + 8 : band_cols * j + 16]
            tile_out[j] = jnp.where(low, top, pltpu.roll(bottom, 2 * band_rows, 1))

    with jax.named_scope("tiles"):

        @pl.loop(0, count)
        def _(step):
            other = lax.rem(col + count // 2 + step, count)
            target = side * count + other

            @pl.when(target != col)
            def _():
                pltpu.make_async_remote_copy(
                    src_ref=tile_out.at[other],
                    dst_ref=tile_in.at[z],
                    send_sem=tile_sent,
                    recv_sem=tile_got,
                    device_id=(row, target),
                    device_id_type=MESH,
                ).start()

            @pl.when(target == col)
            def _():
                pltpu.make_async_copy(tile_out.at[other], tile_in.at[z], tile_got).start()

        wait_for(tile_in, tile_got)
        total = tile_in[0]
        for i in range(1, depth):
            total = total + tile_in[i]
        for i in range(2):
            for s in range(2):
                at = (2 * i + s) * band_rows
                out_ref[s, 8 * i : 8 * i + 8, :] = diag_ref[s, 8 * i : 8 * i + 8, :] + total[:, at : at + band_rows]

    with jax.named_scope("drain"):
        for i in (1, 2, 3):
            anc_copy(i).wait_send()
            far_copy(i).wait_send()

        @pl.when(own_slab)
        def _():
            wait_for(slab.at[pl.ds(0, 4 * rows - 1)], slab_sent)

        @pl.when(jnp.logical_not(own_slab))
        def _():
            wait_for(slab, slab_sent)

        wait_for(left_in.at[pl.ds(0, plane - 1)], left_sent)
        wait_for(kept_in.at[pl.ds(0, plane - 1)], kept_sent)
        wait_for(shares.at[pl.ds(0, plane - 1)], share_sent)
        wait_for(gather_in.at[pl.ds(0, rows - 1)], gather_sent)
        swap.wait_send()

        @pl.when(own)
        def _():
            wait_for(tile_in.at[pl.ds(0, count - 1)], tile_sent)

        @pl.when(jnp.logical_not(own))
        def _():
            wait_for(tile_in, tile_sent)


def local(rows, cols, ancestor_inverse, pattern, listed, panels, parent_panels, diag_inverse):
    supers, height, width = panels.shape
    tall, wide = ancestor_inverse.shape
    depth = cols // 2
    plane = 2 * rows
    half = width // 2
    count = cols // 2
    vmem = pl.BlockSpec(memory_space=pltpu.VMEM)
    smem = pl.BlockSpec(memory_space=pltpu.SMEM)
    anywhere = pl.BlockSpec(memory_space=pl.ANY)
    turned = jnp.swapaxes(diag_inverse, 1, 2)
    upper, tiles = pl.pallas_call(
        functools.partial(kernel, rows, cols),
        out_shape=(
            jax.ShapeDtypeStruct(panels.shape, F32),
            jax.ShapeDtypeStruct(turned.shape, F32),
        ),
        in_specs=[anywhere, smem, smem, anywhere, anywhere, anywhere],
        out_specs=(vmem, vmem),
        scratch_shapes=[
            pltpu.VMEM(ancestor_inverse.shape, F32),
            pltpu.VMEM(panels.shape, F32),
            pltpu.VMEM((width, width), F32),
            pltpu.VMEM(turned.shape, F32),
            pltpu.VMEM((depth // 4, supers, height, width), F32),
            pltpu.VMEM((2, 2 * tall, wide), F32),
            pltpu.VMEM((4 * rows, height, half), F32),
            pltpu.VMEM((plane, height, half), F32),
            pltpu.VMEM((plane, height, half), F32),
            pltpu.VMEM((rows, height, 2 * LANES), F32),
            pltpu.VMEM((plane, height, 2 * LANES), F32),
            pltpu.VMEM((2, height, half), F32),
            pltpu.VMEM((plane, height, half), F32),
            pltpu.VMEM((2, height, width + half), F32),
            pltpu.VMEM((plane, height, width + half), F32),
            pltpu.VMEM((count, 8, LANES), F32),
            pltpu.VMEM((depth, 8, LANES), F32),
            pltpu.SemaphoreType.DMA((4,)),
            pltpu.SemaphoreType.DMA((3,)),
            pltpu.SemaphoreType.DMA((3,)),
            pltpu.SemaphoreType.DMA((3,)),
            pltpu.SemaphoreType.DMA((3,)),
            pltpu.SemaphoreType.DMA((14,)),
        ],
        compiler_params=pltpu.CompilerParams(
            collective_id=0, has_side_effects=True, vmem_limit_bytes=56 * 1024 * 1024
        ),
    )(ancestor_inverse, pattern, listed, panels, parent_panels[0], turned)
    return upper, jnp.swapaxes(tiles, 1, 2)


def solution(mesh):
    rows, cols = mesh.shape["row"], mesh.shape["col"]
    return jax.shard_map(
        functools.partial(local, rows, cols),
        mesh=mesh,
        in_specs=(
            P("row", "col"),
            P(),
            P(),
            P(None, ("col", "row"), None),
            P(),
            P(None, "row", "col"),
        ),
        out_specs=(P(None, ("col", "row"), None), P(None, "row", "col")),
        check_vma=False,
    )
```

time: 85.3 us -> 70.4 us (0.83); the launches traced: 83.6 us -> 70.1 us
  Pallas kernels: 78.7 us -> 67.4 us
  local copies, waits for them, and re-layouts: 4.24 us -> 1.99 us
    pallas_call x1, Pallas kernels: 78.7 us -> 67.4 us  [local(): pl.pallas_call(functools.partial(kernel, rows, cols), out_shape=(jax.Shap...]
    unnamed x12 -> x4, local copies, waits for them, and re-layouts: 3.56 us -> 1.99 us
where the time goes in v2:
time: 70.4 us; the launch traced here: 70.1 us
  Pallas kernels  67.4 us (96%)
  local copies, waits for them, and re-layouts  1.99 us (3%)
    pallas_call x1, Pallas kernels, local(): pl.pallas_call(functools.partial(kernel, rows, cols), out_shape=(jax.Shap...  67.4 us
    unnamed x4, local copies, waits for them, and re-layouts  1.99 us

profile of v2, /device:TPU:1, one launch (start us, length us, event | category | flops | bytes accessed | tf_op | source)
XLA Modules:
  0.0 70.1 jit_solution(15865026456345309025)
XLA Ops:
  0.6 67.4 %shard_map.77 = (f32[2,8,512]{2,1,0:T(8,128)}, f32[2,16,32]{2,1,0:T(8,128)}) custom-call(f32[256,128]{1,0:T(8,128)} %a_hbm.1, s32[32,32]{1,0:T(8,128)} %pattern_ref.1, s32[2,16]{1,0:T(2,128)} %listed_ref.1, f32[2,8,512]{2,1,0:T(8,128)} %panel_hbm.1, f32[512,512]{1,0:T(8,128)} %bitcast.3, f32[2,16,32]{2,1,0:T(8,128)} %bitcast.4), custom_call_target="tpu_custom_call" | custom-call | tf_op jit(solution)/shard_map/pallas_call | solution.py:480
  68.1 0.0 copy-start
  68.1 1.4 %copy.10 = f32[2,8,512]{2,1,0:T(8,128)} copy(f32[2,8,512]{2,1,0:T(8,128)} %get-tuple-element.8) | data formatting | bytes 65536
  69.5 0.0 copy-done
  69.5 0.6 copy.11
Async XLA Ops:
  68.1 1.4 %copy-start = (f32[2,16,32]{2,1,0:T(8,128)S(1)}, f32[2,16,32]{2,1,0:T(8,128)}, u32[]{:S(2)}) copy-start(f32[2,16,32]{2,1,0:T(8,128)} %get-tuple-element.5) | copy-start | bytes 12292

commit v3 on v2

--- a/solution.py
+++ b/solution.py
@@ -9,6 +9,7 @@
 
 BLK = 128
 LANES = 128
+STRIDE = 5
 MESH = pl.DeviceIdType.MESH
 F32 = jnp.float32
 
@@ -25,6 +26,18 @@
         precision=lax.Precision.HIGHEST,
         preferred_element_type=F32,
     )
+
+
+def split(value):
+    high = value.astype(jnp.bfloat16)
+    return high, (value - high.astype(F32)).astype(jnp.bfloat16)
+
+
+def dot_split(left, right, dim=1):
+    def once(a, b):
+        return lax.dot_general(a, b, (((dim,), (0,)), ((), ())), preferred_element_type=F32)
+
+    return once(left[0], right[1]) + once(left[1], right[0]) + once(left[0], right[0])
 
 
 def exchange(parts, width):
@@ -71,11 +84,14 @@
     gather_in,
     tile_out,
     tile_in,
+    extra_out,
+    extra_in,
     load_sems,
     anc_send,
     anc_recv,
     far_send,
     far_recv,
+    gather_got,
     sems,
 ):
     row, col = lax.axis_index("row"), lax.axis_index("col")
@@ -94,12 +110,12 @@
     band_cols = width // cols
     count = cols // 2
     own = lax.div(col, count) == side
-    own_slab = lax.rem(lax.div(z, 2), 2) == lax.rem(pair, 2)
 
     (slab_sent, slab_got, left_sent, left_got, kept_sent, kept_got, share_sent, share_got) = (
         sems.at[i] for i in range(8)
     )
-    gather_sent, gather_got, pass_sent, pass_got, tile_sent, tile_got = (sems.at[i] for i in range(8, 14))
+    gather_sent, pass_sent, pass_got, tile_sent, tile_got = (sems.at[i] for i in range(8, 13))
+    extra_sent, extra_got, forward_sent, forward_got = (sems.at[i] for i in range(13, 17))
 
     def wait_for(ref, sem):
         pltpu.make_async_copy(ref, ref, sem).wait()
@@ -113,9 +129,14 @@
     def plane_at(offset):
         return lax.rem(z + depth + offset, depth)
 
-    def near(residue, core_from):
-        gap = lax.rem(residue, 4)
-        return jnp.where(gap == 3, -1, jnp.where(gap == 2, 2 - 4 * core_from, gap))
+    def holder(block):
+        gap = lax.rem(z + depth - block, depth)
+        back = jnp.where(gap <= 2, 0, jnp.where(gap <= depth // 2, STRIDE, depth - STRIDE))
+        back = jnp.where(gap >= depth - 2, 0, back)
+        return lax.rem(block + back, depth)
+
+    held = [(0, (2, -2, 1, -1, 0)), (-STRIDE, (3, 2, -2, 1, -1, 0)), (STRIDE, (2, -2, 1, -1, 0))]
+    own_slab = functools.reduce(jnp.logical_or, [lax.div(plane_at(offset), 2) == pair for offset, _ in held])
 
     loads = [
         pltpu.make_async_copy(panel_hbm, panel_ref, load_sems.at[0]),
@@ -131,32 +152,23 @@
         def greet(device):
             pl.semaphore_signal(barrier, inc=1, device_id=device, device_id_type=MESH)
 
-        for far in (2, 1, 3):
-            greet((row, lax.rem(col + 8 * far, cols)))
-
-        @pl.loop(0, depth)
-        def _(step):
-            source = 2 * plane_at(step) + lax.div(col, count)
-
-            @pl.when(source != col)
-            def _():
-                greet((row, source))
+        for far in (STRIDE, -STRIDE):
+            greet((row, lax.rem(col + cols + 2 * far, cols)))
 
         @pl.loop(0, plane)
         def _(step):
             other = peer(step)
             row_from, side_from = lax.rem(other, rows), lax.div(other, rows)
-
-            @pl.when(step > 0)
-            def _():
-                greet(place(other))
-
             for i in range(2):
-                offset = near(z + depth - lax.rem(2 * pair + i, 4), lax.rem(row_from, 2))
-
-                @pl.when(jnp.logical_or(step > 0, offset != 0))
+                source = holder(2 * pair + i)
+
+                @pl.when(jnp.logical_or(step > 0, source != z))
                 def _():
-                    greet((row_from, 2 * plane_at(-offset) + side_from))
+                    greet((row_from, 2 * source + side_from))
+
+        @pl.loop(1, plane)
+        def _(step):
+            greet(place(peer(step)))
 
         def keep(s):
             found = listed_ref[s, 0] == col
@@ -168,38 +180,45 @@
         loads[0].wait()
         kept0 = panel_ref[0] * flag0
         kept1 = panel_ref[1] * flag1
-        panels[lax.div(z, 4), 0] = kept0
-        panels[lax.div(z, 4), 1] = kept1
+        panels[0, 0] = kept0
+        panels[0, 1] = kept1
         loads[1].wait()
         for i in range(tall // BLK):
             present = pattern_ref[(tall // BLK) * row + i, col].astype(F32)
             anc[side, pl.ds(core * tall + i * BLK, BLK), :] = a_ref[pl.ds(i * BLK, BLK), :] * present
+        for h in range(2):
+            kept_out[h] = kept1[:, h * half : (h + 1) * half]
+        kept_in[slot_me] = kept_out[side]
+        loads[2].wait()
+        loads[3].wait()
+        mixed = kept1 - dot(kept0, link_ref[...])
+        link_band = link_ref[pl.ds(pl.multiple_of(row * band_rows, 8), band_rows), :]
+        extra = dot(diag_ref[0], link_band)
+        for h in range(2):
+            extra_out[h] = extra[h * height : (h + 1) * height]
         slab_targets = 4 * rows - own_slab.astype(jnp.int32)
-        tile_targets = count - own.astype(jnp.int32)
-        pl.semaphore_wait(barrier, plane - 1 + 3 + slab_targets + tile_targets)
+        pl.semaphore_wait(barrier, plane - 1 + 2 + slab_targets)
 
     def far_copy(j):
-        piece = panels.at[lax.div(z, 4)]
         return pltpu.make_async_remote_copy(
-            src_ref=piece,
-            dst_ref=piece,
+            src_ref=panels.at[0],
+            dst_ref=panels.at[j],
             send_sem=far_send.at[j - 1],
             recv_sem=far_recv.at[j - 1],
-            device_id=(row, lax.rem(col + 8 * j, cols)),
+            device_id=(row, lax.rem(col + cols + (2 * STRIDE if j == 1 else -2 * STRIDE), cols)),
             device_id_type=MESH,
         )
 
     def spread(j):
-        block = plane_at(-4 * j)
+        back, offsets = held[j]
+        block = plane_at(back)
         owner = lax.div(block, 2)
         slot = (lax.rem(block, 2) * 2 + side) * rows + row
-        for offset in (2 - 4 * core, 1, -1, 0):
+        for offset in offsets:
             for step in range(4):
                 quarter = lax.rem(2 * core + side + step, 4)
                 super_of, half_of = lax.div(quarter, 2), lax.rem(quarter, 2)
-                source = panels.at[
-                    lax.div(block, 4), super_of, :, pl.ds(pl.multiple_of(half_of * half, LANES), half)
-                ]
+                source = panels.at[j, super_of, :, pl.ds(pl.multiple_of(half_of * half, LANES), half)]
 
                 def send():
                     pltpu.make_async_remote_copy(
@@ -211,7 +230,7 @@
                         device_id_type=MESH,
                     ).start()
 
-                if step == 0 and isinstance(offset, int) and offset == 0:
+                if step == 0 and offset == 0:
                     pl.when(owner != pair)(send)
 
                     @pl.when(owner == pair)
@@ -233,38 +252,58 @@
             device_id_type=MESH,
         )
 
+    def chip_copy(source, target, sent, got):
+        return pltpu.make_async_remote_copy(
+            src_ref=source,
+            dst_ref=target,
+            send_sem=sent,
+            recv_sem=got,
+            device_id=(2 * pair + 1 - core, col),
+            device_id_type=MESH,
+        )
+
+    chip = side * pairs + pair
+
+    def chip_at(step):
+        other = lax.rem(chip + step, rows)
+        return lax.div(other, pairs), (2 * lax.rem(other, pairs) + core, 2 * z + lax.div(other, pairs))
+
     with jax.named_scope("start"):
-        for j in (2, 1, 3):
+        for j in (1, 2):
             far_copy(j).start()
+        extra_swap = chip_copy(extra_out.at[1 - core], extra_in, extra_sent, extra_got)
+        extra_swap.start()
         for i in (1, 2, 3):
             anc_copy(i).start()
         spread(0)
 
     with jax.named_scope("early"):
-        loads[2].wait()
-        loads[3].wait()
-        mixed = kept1 - dot(kept0, link_ref[...])
-        link_band = link_ref[pl.ds(pl.multiple_of(row * band_rows, 8), band_rows), :]
-        extra = dot(diag_ref[0], link_band)
+
+        @pl.loop(1, rows)
+        def _(step):
+            side_to, target = chip_at(step)
+            pltpu.make_async_remote_copy(
+                src_ref=kept_out.at[side_to],
+                dst_ref=kept_in.at[slot_me],
+                send_sem=kept_sent,
+                recv_sem=kept_got,
+                device_id=target,
+                device_id_type=MESH,
+            ).start()
+
+        extra_swap.wait_recv()
+        extra = extra_out[core] + extra_in[...]
         per = LANES // band_rows
         for g in range(width // LANES):
             cut = slice(g * LANES, (g + 1) * LANES)
-            packed = exchange([kept0[:, cut], kept1[:, cut], mixed[:, cut], extra[:height, cut]], band_rows)
+            packed = exchange([kept0[:, cut], kept1[:, cut], mixed[:, cut], extra[:, cut]], band_rows)
             for j in range(per):
-                left_out[g * per + j, :, :LANES] = packed[j]
-                tail = extra[height:, cut]
-                if j:
-                    tail = pltpu.roll(tail, LANES - j * band_rows, 1)
-                left_out[g * per + j, :, LANES:] = tail
-        for h in range(2):
-            kept_out[h] = kept1[:, h * half : (h + 1) * half]
+                left_out[g * per + j] = packed[j]
         left_in[slot_me] = left_out[row]
-        kept_in[slot_me] = kept_out[side]
 
         @pl.loop(1, plane)
         def _(step):
-            other = peer(step)
-            target = place(other)
+            target = place(peer(step))
             pltpu.make_async_remote_copy(
                 src_ref=left_out.at[target[0]],
                 dst_ref=left_in.at[slot_me],
@@ -273,17 +312,9 @@
                 device_id=target,
                 device_id_type=MESH,
             ).start()
-            pltpu.make_async_remote_copy(
-                src_ref=kept_out.at[lax.div(other, rows)],
-                dst_ref=kept_in.at[slot_me],
-                send_sem=kept_sent,
-                recv_sem=kept_got,
-                device_id=target,
-                device_id_type=MESH,
-            ).start()
 
     with jax.named_scope("spread"):
-        for j in (1, 3, 2):
+        for j in (1, 2):
             far_copy(j).wait_recv()
             spread(j)
 
@@ -292,9 +323,9 @@
             anc_copy(i).wait_recv()
         wait_for(slab, slab_got)
     with jax.named_scope("product"):
-        kept_rows = slab[...].reshape(2 * tall, half)
+        kept_rows = split(slab[...].reshape(2 * tall, half))
         for i in range(2):
-            part = dot_rows(anc[i], kept_rows)
+            part = dot_split(split(anc[i]), kept_rows, 0)
             partial[pl.ds(i * rows, rows)] = part.reshape(rows, height, half)
 
     slot = (2 * core + side) * pairs + pair
@@ -314,30 +345,30 @@
             ).start()
 
     with jax.named_scope("linkterm"):
+        wait_for(kept_in.at[pl.ds(0, rows - 1)], kept_got)
+        mine = pl.ds(core * rows, rows)
+        kept_swap = chip_copy(kept_in.at[mine], kept_in.at[mine], forward_sent, forward_got)
+        kept_swap.start()
         wait_for(left_in.at[pl.ds(0, plane - 1)], left_got)
-        wait_for(kept_in.at[pl.ds(0, plane - 1)], kept_got)
-        lefts = left_in[...].reshape(plane * height, 2 * LANES)
-        kept_half = kept_in[...].reshape(plane * height, half)
+        lefts = left_in[...].reshape(plane * height, LANES)
         column_half = pl.ds(pl.multiple_of(side * half, LANES), half)
-        link_half = link_ref[:, column_half]
         group = pl.ds(pl.multiple_of(lax.div(row, per) * LANES, LANES), LANES)
-        link_group = link_ref[:, group]
+        link_half = split(link_ref[:, column_half])
+        link_group = split(link_ref[:, group])
         link_rows = link_ref[pl.ds(pl.multiple_of(z * 2 * band_cols, 8), 2 * band_cols), column_half]
-
-        def repeat(i):
-            return jnp.concatenate(
-                [
-                    link_rows[s * band_cols + i : s * band_cols + i + height]
-                    for _ in range(2)
-                    for s in range(2)
-                    for _ in range(pairs)
-                ],
-                axis=0,
-            )
-
-        constant = pltpu.roll(dot_rows(repeat(0), lefts[:, :LANES]), 2 * band_rows, 1) + pltpu.roll(
-            dot_rows(repeat(height), lefts[:, LANES:]), band_rows, 1
+        repeated = jnp.concatenate(
+            [
+                link_rows[s * band_cols + k * height : s * band_cols + (k + 1) * height]
+                for k in range(2)
+                for s in range(2)
+                for _ in range(pairs)
+            ],
+            axis=0,
         )
+        constant = pltpu.roll(dot_rows(repeated, lefts), 2 * band_rows, 1)
+        first = split(lefts)
+        kept_swap.wait_recv()
+        kept_half = split(kept_in[...].reshape(plane * height, half))
 
     with jax.named_scope("shares"):
         wait_for(shares.at[pl.ds(0, plane - 1)], share_got)
@@ -356,51 +387,47 @@
         gather_in[slot_me] = gather_out[side]
 
     with jax.named_scope("gather"):
-        chip = side * pairs + pair
 
         @pl.loop(1, rows)
         def _(step):
-            other = lax.rem(chip + step, rows)
+            side_to, target = chip_at(step)
             pltpu.make_async_remote_copy(
-                src_ref=gather_out.at[lax.div(other, pairs)],
+                src_ref=gather_out.at[side_to],
                 dst_ref=gather_in.at[slot_me],
                 send_sem=gather_sent,
-                recv_sem=gather_got,
-                device_id=(2 * lax.rem(other, pairs) + core, 2 * z + lax.div(other, pairs)),
+                recv_sem=gather_got.at[step],
+                device_id=target,
                 device_id_type=MESH,
             ).start()
 
+        chip_copy(gather_in.at[slot_me], gather_in.at[slot_me], pass_sent, pass_got).start()
         upper_ref[0] = upper0
         upper_ref[1] = -(sum1 + dot(upper0, link_ref[...])) * flag1
-        wait_for(gather_in.at[pl.ds(0, rows - 1)], gather_got)
-        mine = gather_in.at[pl.ds(core * rows, rows)]
-        swap = pltpu.make_async_remote_copy(
-            src_ref=mine,
-            dst_ref=mine,
-            send_sem=pass_sent,
-            recv_sem=pass_got,
-            device_id=(2 * pair + 1 - core, col),
-            device_id_type=MESH,
-        )
-        swap.start()
-        swap.wait_recv()
+
+        @pl.loop(1, rows)
+        def _(step):
+            slot_from = core * rows + lax.rem(chip + rows - step, rows)
+            arrived = gather_in.at[slot_from]
+            wait_for(arrived, gather_got.at[step])
+            chip_copy(arrived, arrived, pass_sent, pass_got).start()
+
+        wait_for(gather_in.at[mine], pass_got)
 
     with jax.named_scope("diagonal"):
-        uppers = gather_in[:, :, :width].reshape(plane * height, width)
-        sums = gather_in[:, :, width:].reshape(plane * height, half)
-        chained_half = dot(uppers, link_half)
-        chained_group = dot(uppers, link_group)
-        upper_half = gather_in[:, :, column_half].reshape(plane * height, half)
-        first = lefts[:, :LANES]
+        uppers = split(gather_in[:, :, :width].reshape(plane * height, width))
+        sums = split(gather_in[:, :, width:].reshape(plane * height, half))
+        chained_half = split(dot_split(uppers, link_half))
+        chained_group = split(dot_split(uppers, link_group))
+        upper_half = split(gather_in[:, :, column_half].reshape(plane * height, half))
         turn = lax.rem(LANES + band_rows - lax.rem(row, per) * band_rows, LANES)
         later = (
-            dot_rows(sums, first)
-            + pltpu.roll(dot_rows(chained_half, first), LANES - band_rows, 1)
-            + pltpu.roll(dot_rows(kept_half, chained_group), turn, 1)
+            dot_split(sums, first, 0)
+            + pltpu.roll(dot_split(chained_half, first, 0), LANES - band_rows, 1)
+            + pltpu.roll(dot_split(kept_half, chained_group, 0), turn, 1)
             + constant
         )
         lane = lax.broadcasted_iota(jnp.int32, (half, LANES), 1)
-        tiles = jnp.where(lane < band_rows, -dot_rows(upper_half, first), later)
+        tiles = jnp.where(lane < band_rows, -dot_split(upper_half, first, 0), later)
         low = lane[:8] < 2 * band_rows
         for j in range(count):
             top = tiles[band_cols * j : band_cols * j + 8]
@@ -441,7 +468,10 @@
     with jax.named_scope("drain"):
         for i in (1, 2, 3):
             anc_copy(i).wait_send()
-            far_copy(i).wait_send()
+        for j in (1, 2):
+            far_copy(j).wait_send()
+        extra_swap.wait_send()
+        kept_swap.wait_send()
 
         @pl.when(own_slab)
         def _():
@@ -452,10 +482,10 @@
             wait_for(slab, slab_sent)
 
         wait_for(left_in.at[pl.ds(0, plane - 1)], left_sent)
-        wait_for(kept_in.at[pl.ds(0, plane - 1)], kept_sent)
+        wait_for(kept_in.at[pl.ds(0, rows - 1)], kept_sent)
         wait_for(shares.at[pl.ds(0, plane - 1)], share_sent)
         wait_for(gather_in.at[pl.ds(0, rows - 1)], gather_sent)
-        swap.wait_send()
+        wait_for(gather_in.at[mine], pass_sent)
 
         @pl.when(own)
         def _():
@@ -490,25 +520,28 @@
             pltpu.VMEM(panels.shape, F32),
             pltpu.VMEM((width, width), F32),
             pltpu.VMEM(turned.shape, F32),
-            pltpu.VMEM((depth // 4, supers, height, width), F32),
+            pltpu.VMEM((3, supers, height, width), F32),
             pltpu.VMEM((2, 2 * tall, wide), F32),
             pltpu.VMEM((4 * rows, height, half), F32),
             pltpu.VMEM((plane, height, half), F32),
             pltpu.VMEM((plane, height, half), F32),
-            pltpu.VMEM((rows, height, 2 * LANES), F32),
-            pltpu.VMEM((plane, height, 2 * LANES), F32),
+            pltpu.VMEM((rows, height, LANES), F32),
+            pltpu.VMEM((plane, height, LANES), F32),
             pltpu.VMEM((2, height, half), F32),
             pltpu.VMEM((plane, height, half), F32),
             pltpu.VMEM((2, height, width + half), F32),
             pltpu.VMEM((plane, height, width + half), F32),
             pltpu.VMEM((count, 8, LANES), F32),
             pltpu.VMEM((depth, 8, LANES), F32),
+            pltpu.VMEM((2, height, width), F32),
+            pltpu.VMEM((height, width), F32),
             pltpu.SemaphoreType.DMA((4,)),
             pltpu.SemaphoreType.DMA((3,)),
             pltpu.SemaphoreType.DMA((3,)),
-            pltpu.SemaphoreType.DMA((3,)),
-            pltpu.SemaphoreType.DMA((3,)),
-            pltpu.SemaphoreType.DMA((14,)),
+            pltpu.SemaphoreType.DMA((2,)),
+            pltpu.SemaphoreType.DMA((2,)),
+            pltpu.SemaphoreType.DMA((rows,)),
+            pltpu.SemaphoreType.DMA((17,)),
         ],
         compiler_params=pltpu.CompilerParams(
             collective_id=0, has_side_effects=True, vmem_limit_bytes=56 * 1024 * 1024

time: 70.4 us -> 67 us (0.952)
  the two profiles are of different devices: /device:TPU:1 before, /device:TPU:35 now
where the time goes in v3:
time: 67 us; the launch traced here: 66.7 us
  Pallas kernels  64.1 us (96%)
  local copies, waits for them, and re-layouts  1.99 us (3%)
    pallas_call x1, Pallas kernels, local(): pl.pallas_call(functools.partial(kernel, rows, cols), out_shape=(jax.Shap...  64.1 us
    unnamed x4, local copies, waits for them, and re-layouts  1.99 us

profile of v3, /device:TPU:35, one launch (start us, length us, event | category | flops | bytes accessed | tf_op | source)
XLA Modules:
  0.0 66.7 jit_solution(6202871327319530890)
XLA Ops:
  0.6 64.1 %shard_map.77 = (f32[2,8,512]{2,1,0:T(8,128)}, f32[2,16,32]{2,1,0:T(8,128)}) custom-call(f32[256,128]{1,0:T(8,128)} %a_hbm.1, s32[32,32]{1,0:T(8,128)} %pattern_ref.1, s32[2,16]{1,0:T(2,128)} %listed_ref.1, f32[2,8,512]{2,1,0:T(8,128)} %panel_hbm.1, f32[512,512]{1,0:T(8,128)} %bitcast.3, f32[2,16,32]{2,1,0:T(8,128)} %bitcast.4), custom_call_target="tpu_custom_call" | custom-call | tf_op jit(solution)/shard_map/pallas_call | solution.py:510
  64.7 0.0 copy-start
  64.7 1.4 %copy.10 = f32[2,8,512]{2,1,0:T(8,128)} copy(f32[2,8,512]{2,1,0:T(8,128)} %get-tuple-element.8) | data formatting | bytes 65536
  66.1 0.0 copy-done
  66.1 0.6 copy.11
Async XLA Ops:
  64.7 1.4 %copy-start = (f32[2,16,32]{2,1,0:T(8,128)S(1)}, f32[2,16,32]{2,1,0:T(8,128)}, u32[]{:S(2)}) copy-start(f32[2,16,32]{2,1,0:T(8,128)} %get-tuple-element.5) | copy-start | bytes 12292

commit v4 on v3

--- a/solution.py
+++ b/solution.py
@@ -10,6 +10,7 @@
 BLK = 128
 LANES = 128
 STRIDE = 5
+HOPS = (3, 2, -2, 1, -1)
 MESH = pl.DeviceIdType.MESH
 F32 = jnp.float32
 
@@ -92,6 +93,7 @@
     far_send,
     far_recv,
     gather_got,
+    ready,
     sems,
 ):
     row, col = lax.axis_index("row"), lax.axis_index("col")
@@ -120,22 +122,31 @@
     def wait_for(ref, sem):
         pltpu.make_async_copy(ref, ref, sem).wait()
 
-    def place(index):
-        return (lax.rem(index, rows), 2 * z + lax.div(index, rows))
-
-    def peer(step):
-        return lax.rem(me + step, plane)
+    def wrap(value, size):
+        return jnp.where(value >= size, value - size, value)
 
     def plane_at(offset):
-        return lax.rem(z + depth + offset, depth)
-
-    def holder(block):
-        gap = lax.rem(z + depth - block, depth)
-        back = jnp.where(gap <= 2, 0, jnp.where(gap <= depth // 2, STRIDE, depth - STRIDE))
-        back = jnp.where(gap >= depth - 2, 0, back)
-        return lax.rem(block + back, depth)
-
-    held = [(0, (2, -2, 1, -1, 0)), (-STRIDE, (3, 2, -2, 1, -1, 0)), (STRIDE, (2, -2, 1, -1, 0))]
+        return wrap(z + offset % depth, depth)
+
+    def each_peer(act):
+        act(row, 1 - side)
+
+        @pl.loop(1, rows)
+        def _(step):
+            other = wrap(row + step, rows)
+            act(other, side)
+            act(other, 1 - side)
+
+    def each_chip(act):
+        act(pair, 1 - side, 1)
+
+        @pl.loop(1, pairs)
+        def _(step):
+            other = wrap(pair + step, pairs)
+            act(other, side, 2 * step)
+            act(other, 1 - side, 2 * step + 1)
+
+    held = [(0, (*HOPS[1:], 0)), (-STRIDE, (*HOPS, 0)), (STRIDE, (*HOPS[1:], 0))]
     own_slab = functools.reduce(jnp.logical_or, [lax.div(plane_at(offset), 2) == pair for offset, _ in held])
 
     loads = [
@@ -152,23 +163,9 @@
         def greet(device):
             pl.semaphore_signal(barrier, inc=1, device_id=device, device_id_type=MESH)
 
-        for far in (STRIDE, -STRIDE):
-            greet((row, lax.rem(col + cols + 2 * far, cols)))
-
-        @pl.loop(0, plane)
-        def _(step):
-            other = peer(step)
-            row_from, side_from = lax.rem(other, rows), lax.div(other, rows)
-            for i in range(2):
-                source = holder(2 * pair + i)
-
-                @pl.when(jnp.logical_or(step > 0, source != z))
-                def _():
-                    greet((row_from, 2 * source + side_from))
-
-        @pl.loop(1, plane)
-        def _(step):
-            greet(place(peer(step)))
+        for offset in (*HOPS, STRIDE, -STRIDE):
+            greet((row, 2 * plane_at(offset) + side))
+        each_peer(lambda r, s: greet((r, 2 * z + s)))
 
         def keep(s):
             found = listed_ref[s, 0] == col
@@ -186,18 +183,7 @@
         for i in range(tall // BLK):
             present = pattern_ref[(tall // BLK) * row + i, col].astype(F32)
             anc[side, pl.ds(core * tall + i * BLK, BLK), :] = a_ref[pl.ds(i * BLK, BLK), :] * present
-        for h in range(2):
-            kept_out[h] = kept1[:, h * half : (h + 1) * half]
-        kept_in[slot_me] = kept_out[side]
-        loads[2].wait()
-        loads[3].wait()
-        mixed = kept1 - dot(kept0, link_ref[...])
-        link_band = link_ref[pl.ds(pl.multiple_of(row * band_rows, 8), band_rows), :]
-        extra = dot(diag_ref[0], link_band)
-        for h in range(2):
-            extra_out[h] = extra[h * height : (h + 1) * height]
-        slab_targets = 4 * rows - own_slab.astype(jnp.int32)
-        pl.semaphore_wait(barrier, plane - 1 + 2 + slab_targets)
+        pl.semaphore_wait(barrier, plane - 1 + len(HOPS) + 2)
 
     def far_copy(j):
         return pltpu.make_async_remote_copy(
@@ -205,7 +191,7 @@
             dst_ref=panels.at[j],
             send_sem=far_send.at[j - 1],
             recv_sem=far_recv.at[j - 1],
-            device_id=(row, lax.rem(col + cols + (2 * STRIDE if j == 1 else -2 * STRIDE), cols)),
+            device_id=(row, 2 * plane_at(STRIDE if j == 1 else -STRIDE) + side),
             device_id_type=MESH,
         )
 
@@ -216,8 +202,8 @@
         slot = (lax.rem(block, 2) * 2 + side) * rows + row
         for offset in offsets:
             for step in range(4):
-                quarter = lax.rem(2 * core + side + step, 4)
-                super_of, half_of = lax.div(quarter, 2), lax.rem(quarter, 2)
+                super_of = core if step < 2 else 1 - core
+                half_of = side if step % 2 == 0 else 1 - side
                 source = panels.at[j, super_of, :, pl.ds(pl.multiple_of(half_of * half, LANES), half)]
 
                 def send():
@@ -240,8 +226,8 @@
                     send()
 
     def anc_copy(i):
-        other_row = 2 * pair + (core + i) % 2
-        other_col = 2 * z + (side + i // 2) % 2
+        other_row = row if i == 2 else 2 * pair + 1 - core
+        other_col = col if i == 1 else 2 * z + 1 - side
         piece = anc.at[side, pl.ds(core * tall, tall), :]
         return pltpu.make_async_remote_copy(
             src_ref=piece,
@@ -262,35 +248,43 @@
             device_id_type=MESH,
         )
 
-    chip = side * pairs + pair
-
-    def chip_at(step):
-        other = lax.rem(chip + step, rows)
-        return lax.div(other, pairs), (2 * lax.rem(other, pairs) + core, 2 * z + lax.div(other, pairs))
-
     with jax.named_scope("start"):
         for j in (1, 2):
             far_copy(j).start()
-        extra_swap = chip_copy(extra_out.at[1 - core], extra_in, extra_sent, extra_got)
-        extra_swap.start()
+        for offset in HOPS:
+            pl.semaphore_signal(
+                ready, inc=1, device_id=(row, 2 * plane_at(-offset) + side), device_id_type=MESH
+            )
         for i in (1, 2, 3):
             anc_copy(i).start()
-        spread(0)
 
     with jax.named_scope("early"):
-
-        @pl.loop(1, rows)
-        def _(step):
-            side_to, target = chip_at(step)
+        for h in range(2):
+            kept_out[h] = kept1[:, h * half : (h + 1) * half]
+        kept_in[slot_me] = kept_out[side]
+
+        def send_kept(p, s, _):
             pltpu.make_async_remote_copy(
-                src_ref=kept_out.at[side_to],
+                src_ref=kept_out.at[s],
                 dst_ref=kept_in.at[slot_me],
                 send_sem=kept_sent,
                 recv_sem=kept_got,
-                device_id=target,
+                device_id=(2 * p + core, 2 * z + s),
                 device_id_type=MESH,
             ).start()
 
+        loads[2].wait()
+        loads[3].wait()
+        mixed = kept1 - dot(kept0, link_ref[...])
+        link_band = link_ref[pl.ds(pl.multiple_of(row * band_rows, 8), band_rows), :]
+        extra = dot(diag_ref[0], link_band)
+        for h in range(2):
+            extra_out[h] = extra[h * height : (h + 1) * height]
+        extra_swap = chip_copy(extra_out.at[1 - core], extra_in, extra_sent, extra_got)
+        extra_swap.start()
+        pl.semaphore_wait(ready, len(HOPS))
+        spread(0)
+        each_chip(send_kept)
         extra_swap.wait_recv()
         extra = extra_out[core] + extra_in[...]
         per = LANES // band_rows
@@ -301,15 +295,14 @@
                 left_out[g * per + j] = packed[j]
         left_in[slot_me] = left_out[row]
 
-        @pl.loop(1, plane)
-        def _(step):
-            target = place(peer(step))
+        @each_peer
+        def _(r, s):
             pltpu.make_async_remote_copy(
-                src_ref=left_out.at[target[0]],
+                src_ref=left_out.at[r],
                 dst_ref=left_in.at[slot_me],
                 send_sem=left_sent,
                 recv_sem=left_got,
-                device_id=target,
+                device_id=(r, 2 * z + s),
                 device_id_type=MESH,
             ).start()
 
@@ -332,15 +325,14 @@
     with jax.named_scope("scatter"):
         shares[slot] = partial[me]
 
-        @pl.loop(1, plane)
-        def _(step):
-            other = peer(step)
+        @each_peer
+        def _(r, s):
             pltpu.make_async_remote_copy(
-                src_ref=partial.at[other],
+                src_ref=partial.at[s * rows + r],
                 dst_ref=shares.at[slot],
                 send_sem=share_sent,
                 recv_sem=share_got,
-                device_id=place(other),
+                device_id=(r, 2 * z + s),
                 device_id_type=MESH,
             ).start()
 
@@ -388,15 +380,14 @@
 
     with jax.named_scope("gather"):
 
-        @pl.loop(1, rows)
-        def _(step):
-            side_to, target = chip_at(step)
+        @each_chip
+        def _(p, s, number):
             pltpu.make_async_remote_copy(
-                src_ref=gather_out.at[side_to],
+                src_ref=gather_out.at[s],
                 dst_ref=gather_in.at[slot_me],
                 send_sem=gather_sent,
-                recv_sem=gather_got.at[step],
-                device_id=target,
+                recv_sem=gather_got.at[number],
+                device_id=(2 * p + core, 2 * z + s),
                 device_id_type=MESH,
             ).start()
 
@@ -404,12 +395,18 @@
         upper_ref[0] = upper0
         upper_ref[1] = -(sum1 + dot(upper0, link_ref[...])) * flag1
 
-        @pl.loop(1, rows)
+        def forward(p, s, number):
+            arrived = gather_in.at[(core * 2 + s) * pairs + p]
+            wait_for(arrived, gather_got.at[number])
+            chip_copy(arrived, arrived, pass_sent, pass_got).start()
+
+        forward(pair, 1 - side, 1)
+
+        @pl.loop(1, pairs)
         def _(step):
-            slot_from = core * rows + lax.rem(chip + rows - step, rows)
-            arrived = gather_in.at[slot_from]
-            wait_for(arrived, gather_got.at[step])
-            chip_copy(arrived, arrived, pass_sent, pass_got).start()
+            other = wrap(pair + pairs - step, pairs)
+            forward(other, side, 2 * step)
+            forward(other, 1 - side, 2 * step + 1)
 
         wait_for(gather_in.at[mine], pass_got)
 
@@ -436,13 +433,10 @@
 
     with jax.named_scope("tiles"):
 
-        @pl.loop(0, count)
-        def _(step):
-            other = lax.rem(col + count // 2 + step, count)
+        for other in range(count):
             target = side * count + other
 
-            @pl.when(target != col)
-            def _():
+            def send():
                 pltpu.make_async_remote_copy(
                     src_ref=tile_out.at[other],
                     dst_ref=tile_in.at[z],
@@ -451,6 +445,8 @@
                     device_id=(row, target),
                     device_id_type=MESH,
                 ).start()
+
+            pl.when(target != col)(send)
 
             @pl.when(target == col)
             def _():
@@ -541,6 +537,7 @@
             pltpu.SemaphoreType.DMA((2,)),
             pltpu.SemaphoreType.DMA((2,)),
             pltpu.SemaphoreType.DMA((rows,)),
+            pltpu.SemaphoreType.REGULAR,
             pltpu.SemaphoreType.DMA((17,)),
         ],
         compiler_params=pltpu.CompilerParams(

time: 67 us -> 64.3 us (0.960)
  Pallas kernels: 64.1 us -> 61.4 us
    pallas_call x1, Pallas kernels: 64.1 us -> 61.4 us  [local(): pl.pallas_call(functools.partial(kernel, rows, cols), out_shape=(jax.Shap...]
where the time goes in v4:
time: 64.3 us; the launch traced here: 64.1 us
  Pallas kernels  61.4 us (95%)
  local copies, waits for them, and re-layouts  1.99 us (3%)
  between operations  0.65 us (1%)
    pallas_call x1, Pallas kernels, local(): pl.pallas_call(functools.partial(kernel, rows, cols), out_shape=(jax.Shap...  61.4 us
    unnamed x4, local copies, waits for them, and re-layouts  1.99 us

profile of v4, /device:TPU:35, one launch (start us, length us, event | category | flops | bytes accessed | tf_op | source)
XLA Modules:
  0.0 64.1 jit_solution(17955649490115270026)
XLA Ops:
  0.6 61.4 %shard_map.77 = (f32[2,8,512]{2,1,0:T(8,128)}, f32[2,16,32]{2,1,0:T(8,128)}) custom-call(f32[256,128]{1,0:T(8,128)} %a_hbm.1, s32[32,32]{1,0:T(8,128)} %pattern_ref.1, s32[2,16]{1,0:T(2,128)} %listed_ref.1, f32[2,8,512]{2,1,0:T(8,128)} %panel_hbm.1, f32[512,512]{1,0:T(8,128)} %bitcast.3, f32[2,16,32]{2,1,0:T(8,128)} %bitcast.4), custom_call_target="tpu_custom_call" | custom-call | tf_op jit(solution)/shard_map/pallas_call | solution.py:506
  62.1 0.0 copy-start
  62.1 1.4 %copy.10 = f32[2,8,512]{2,1,0:T(8,128)} copy(f32[2,8,512]{2,1,0:T(8,128)} %get-tuple-element.8) | data formatting | bytes 65536
  63.4 0.0 copy-done
  63.4 0.6 copy.11
Async XLA Ops:
  62.1 1.4 %copy-start = (f32[2,16,32]{2,1,0:T(8,128)S(1)}, f32[2,16,32]{2,1,0:T(8,128)}, u32[]{:S(2)}) copy-start(f32[2,16,32]{2,1,0:T(8,128)} %get-tuple-element.5) | copy-start | bytes 12292

commit v5 on v4

--- a/solution.py
+++ b/solution.py
@@ -226,15 +226,13 @@
                     send()
 
     def anc_copy(i):
-        other_row = row if i == 2 else 2 * pair + 1 - core
-        other_col = col if i == 1 else 2 * z + 1 - side
-        piece = anc.at[side, pl.ds(core * tall, tall), :]
+        piece = anc.at[1 - side if i == 3 else side, pl.ds(core * tall, tall), :]
         return pltpu.make_async_remote_copy(
             src_ref=piece,
             dst_ref=piece,
             send_sem=anc_send.at[i - 1],
             recv_sem=anc_recv.at[i - 1],
-            device_id=(other_row, other_col),
+            device_id=(row, 2 * z + 1 - side) if i == 2 else (2 * pair + 1 - core, col),
             device_id_type=MESH,
         )
 
@@ -255,7 +253,7 @@
             pl.semaphore_signal(
                 ready, inc=1, device_id=(row, 2 * plane_at(-offset) + side), device_id_type=MESH
             )
-        for i in (1, 2, 3):
+        for i in (2, 1):
             anc_copy(i).start()
 
     with jax.named_scope("early"):
@@ -310,9 +308,11 @@
         for j in (1, 2):
             far_copy(j).wait_recv()
             spread(j)
+        anc_copy(2).wait_recv()
+        anc_copy(3).start()
 
     with jax.named_scope("slab"):
-        for i in (1, 2, 3):
+        for i in (1, 3):
             anc_copy(i).wait_recv()
         wait_for(slab, slab_got)
     with jax.named_scope("product"):

time: 64.3 us -> 60.5 us (0.941)
  the two profiles are of different devices: /device:TPU:35 before, /device:TPU:1 now
where the time goes in v5:
time: 60.5 us; the launch traced here: 60.2 us
  Pallas kernels  57.6 us (95%)
  local copies, waits for them, and re-layouts  1.99 us (3%)
  between operations  0.65 us (1%)
    pallas_call x1, Pallas kernels, local(): pl.pallas_call(functools.partial(kernel, rows, cols), out_shape=(jax.Shap...  57.6 us
    unnamed x4, local copies, waits for them, and re-layouts  1.99 us

profile of v5, /device:TPU:1, one launch (start us, length us, event | category | flops | bytes accessed | tf_op | source)
XLA Modules:
  0.0 60.2 jit_solution(1308869624918628847)
XLA Ops:
  0.6 57.6 %shard_map.77 = (f32[2,8,512]{2,1,0:T(8,128)}, f32[2,16,32]{2,1,0:T(8,128)}) custom-call(f32[256,128]{1,0:T(8,128)} %a_hbm.1, s32[32,32]{1,0:T(8,128)} %pattern_ref.1, s32[2,16]{1,0:T(2,128)} %listed_ref.1, f32[2,8,512]{2,1,0:T(8,128)} %panel_hbm.1, f32[512,512]{1,0:T(8,128)} %bitcast.3, f32[2,16,32]{2,1,0:T(8,128)} %bitcast.4), custom_call_target="tpu_custom_call" | custom-call | tf_op jit(solution)/shard_map/pallas_call | solution.py:506
  58.2 0.0 copy-start
  58.3 1.4 %copy.10 = f32[2,8,512]{2,1,0:T(8,128)} copy(f32[2,8,512]{2,1,0:T(8,128)} %get-tuple-element.8) | data formatting | bytes 65536
  59.6 0.0 copy-done
  59.6 0.6 %copy.11 = f32[2,32,16]{1,2,0:T(8,128)} copy(f32[2,32,16]{1,2,0:T(8,128)S(1)} %bitcast.5) | data formatting | bytes 8192
Async XLA Ops:
  58.2 1.4 %copy-start = (f32[2,16,32]{2,1,0:T(8,128)S(1)}, f32[2,16,32]{2,1,0:T(8,128)}, u32[]{:S(2)}) copy-start(f32[2,16,32]{2,1,0:T(8,128)} %get-tuple-element.5) | copy-start | bytes 12292

commit v6 on v5

--- a/solution.py
+++ b/solution.py
@@ -185,25 +185,24 @@
             anc[side, pl.ds(core * tall + i * BLK, BLK), :] = a_ref[pl.ds(i * BLK, BLK), :] * present
         pl.semaphore_wait(barrier, plane - 1 + len(HOPS) + 2)
 
-    def far_copy(j):
+    def far_copy(j, super_of):
         return pltpu.make_async_remote_copy(
-            src_ref=panels.at[0],
-            dst_ref=panels.at[j],
-            send_sem=far_send.at[j - 1],
-            recv_sem=far_recv.at[j - 1],
+            src_ref=panels.at[0, super_of],
+            dst_ref=panels.at[j, super_of],
+            send_sem=far_send.at[j - 1, super_of],
+            recv_sem=far_recv.at[j - 1, super_of],
             device_id=(row, 2 * plane_at(STRIDE if j == 1 else -STRIDE) + side),
             device_id_type=MESH,
         )
 
-    def spread(j):
+    def spread(j, super_of):
         back, offsets = held[j]
         block = plane_at(back)
         owner = lax.div(block, 2)
         slot = (lax.rem(block, 2) * 2 + side) * rows + row
         for offset in offsets:
-            for step in range(4):
-                super_of = core if step < 2 else 1 - core
-                half_of = side if step % 2 == 0 else 1 - side
+            for step in range(2):
+                half_of = side if step == 0 else 1 - side
                 source = panels.at[j, super_of, :, pl.ds(pl.multiple_of(half_of * half, LANES), half)]
 
                 def send():
@@ -217,9 +216,10 @@
                     ).start()
 
                 if step == 0 and offset == 0:
-                    pl.when(owner != pair)(send)
-
-                    @pl.when(owner == pair)
+                    here = jnp.logical_and(owner == pair, core == super_of)
+                    pl.when(jnp.logical_not(here))(send)
+
+                    @pl.when(here)
                     def _():
                         pltpu.make_async_copy(source, slab.at[slot], slab_got).start()
                 else:
@@ -247,8 +247,9 @@
         )
 
     with jax.named_scope("start"):
-        for j in (1, 2):
-            far_copy(j).start()
+        for super_of in range(2):
+            for j in (1, 2):
+                far_copy(j, super_of).start()
         for offset in HOPS:
             pl.semaphore_signal(
                 ready, inc=1, device_id=(row, 2 * plane_at(-offset) + side), device_id_type=MESH
@@ -281,7 +282,8 @@
         extra_swap = chip_copy(extra_out.at[1 - core], extra_in, extra_sent, extra_got)
         extra_swap.start()
         pl.semaphore_wait(ready, len(HOPS))
-        spread(0)
+        for super_of in range(2):
+            spread(0, super_of)
         each_chip(send_kept)
         extra_swap.wait_recv()
         extra = extra_out[core] + extra_in[...]
@@ -305,9 +307,10 @@
             ).start()
 
     with jax.named_scope("spread"):
-        for j in (1, 2):
-            far_copy(j).wait_recv()
-            spread(j)
+        for super_of in range(2):
+            for j in (1, 2):
+                far_copy(j, super_of).wait_recv()
+                spread(j, super_of)
         anc_copy(2).wait_recv()
         anc_copy(3).start()
 
@@ -464,8 +467,9 @@
     with jax.named_scope("drain"):
         for i in (1, 2, 3):
             anc_copy(i).wait_send()
-        for j in (1, 2):
-            far_copy(j).wait_send()
+        for super_of in range(2):
+            for j in (1, 2):
+                far_copy(j, super_of).wait_send()
         extra_swap.wait_send()
         kept_swap.wait_send()
 
@@ -534,8 +538,8 @@
             pltpu.SemaphoreType.DMA((4,)),
             pltpu.SemaphoreType.DMA((3,)),
             pltpu.SemaphoreType.DMA((3,)),
-            pltpu.SemaphoreType.DMA((2,)),
-            pltpu.SemaphoreType.DMA((2,)),
+            pltpu.SemaphoreType.DMA((2, 2)),
+            pltpu.SemaphoreType.DMA((2, 2)),
             pltpu.SemaphoreType.DMA((rows,)),
             pltpu.SemaphoreType.REGULAR,
             pltpu.SemaphoreType.DMA((17,)),

time: 60.5 us -> 60.4 us (level)
  the two profiles are of different devices: /device:TPU:1 before, /device:TPU:39 now
where the time goes in v6:
time: 60.4 us; the launch traced here: 60.1 us
  Pallas kernels  57.5 us (95%)
  local copies, waits for them, and re-layouts  1.99 us (3%)
  between operations  0.65 us (1%)
    pallas_call x1, Pallas kernels, local(): pl.pallas_call(functools.partial(kernel, rows, cols), out_shape=(jax.Shap...  57.5 us
    unnamed x4, local copies, waits for them, and re-layouts  1.99 us

profile of v6, /device:TPU:39, one launch (start us, length us, event | category | flops | bytes accessed | tf_op | source)
XLA Modules:
  0.0 60.1 jit_solution(15801864917744163736)
XLA Ops:
  0.6 57.5 %shard_map.77 = (f32[2,8,512]{2,1,0:T(8,128)}, f32[2,16,32]{2,1,0:T(8,128)}) custom-call(f32[256,128]{1,0:T(8,128)} %a_hbm.1, s32[32,32]{1,0:T(8,128)} %pattern_ref.1, s32[2,16]{1,0:T(2,128)} %listed_ref.1, f32[2,8,512]{2,1,0:T(8,128)} %panel_hbm.1, f32[512,512]{1,0:T(8,128)} %bitcast.3, f32[2,16,32]{2,1,0:T(8,128)} %bitcast.4), custom_call_target="tpu_custom_call" | custom-call | tf_op jit(solution)/shard_map/pallas_call | solution.py:510
  58.1 0.0 copy-start
  58.1 1.4 %copy.10 = f32[2,8,512]{2,1,0:T(8,128)} copy(f32[2,8,512]{2,1,0:T(8,128)} %get-tuple-element.8) | data formatting | bytes 65536
  59.5 0.0 copy-done
  59.5 0.6 %copy.11 = f32[2,32,16]{1,2,0:T(8,128)} copy(f32[2,32,16]{1,2,0:T(8,128)S(1)} %bitcast.5) | data formatting | bytes 8192
Async XLA Ops:
  58.1 1.4 %copy-start = (f32[2,16,32]{2,1,0:T(8,128)S(1)}, f32[2,16,32]{2,1,0:T(8,128)}, u32[]{:S(2)}) copy-start(f32[2,16,32]{2,1,0:T(8,128)} %get-tuple-element.5) | copy-start | bytes 12292

commit v7 on v6

--- a/solution.py
+++ b/solution.py
@@ -87,6 +87,7 @@
     tile_in,
     extra_out,
     extra_in,
+    turned,
     load_sems,
     anc_send,
     anc_recv,
@@ -317,11 +318,13 @@
     with jax.named_scope("slab"):
         for i in (1, 3):
             anc_copy(i).wait_recv()
+        for i in range(2):
+            turned[2 * i], turned[2 * i + 1] = split(anc[i].T)
         wait_for(slab, slab_got)
     with jax.named_scope("product"):
         kept_rows = split(slab[...].reshape(2 * tall, half))
         for i in range(2):
-            part = dot_split(split(anc[i]), kept_rows, 0)
+            part = dot_split((turned[2 * i], turned[2 * i + 1]), kept_rows)
             partial[pl.ds(i * rows, rows)] = part.reshape(rows, height, half)
 
     slot = (2 * core + side) * pairs + pair
@@ -395,8 +398,6 @@
             ).start()
 
         chip_copy(gather_in.at[slot_me], gather_in.at[slot_me], pass_sent, pass_got).start()
-        upper_ref[0] = upper0
-        upper_ref[1] = -(sum1 + dot(upper0, link_ref[...])) * flag1
 
         def forward(p, s, number):
             arrived = gather_in.at[(core * 2 + s) * pairs + p]
@@ -434,7 +435,12 @@
             bottom = tiles[band_cols * j + 8 : band_cols * j + 16]
             tile_out[j] = jnp.where(low, top, pltpu.roll(bottom, 2 * band_rows, 1))
 
+    def finish_upper():
+        upper_ref[0] = upper0
+        upper_ref[1] = -(sum1 + dot(upper0, link_ref[...])) * flag1
+
     with jax.named_scope("tiles"):
+        pl.when(side == 1)(finish_upper)
 
         for other in range(count):
             target = side * count + other
@@ -455,6 +461,7 @@
             def _():
                 pltpu.make_async_copy(tile_out.at[other], tile_in.at[z], tile_got).start()
 
+        pl.when(side == 0)(finish_upper)
         wait_for(tile_in, tile_got)
         total = tile_in[0]
         for i in range(1, depth):
@@ -535,6 +542,7 @@
             pltpu.VMEM((depth, 8, LANES), F32),
             pltpu.VMEM((2, height, width), F32),
             pltpu.VMEM((height, width), F32),
+            pltpu.VMEM((4, wide, 2 * tall), jnp.bfloat16),
             pltpu.SemaphoreType.DMA((4,)),
             pltpu.SemaphoreType.DMA((3,)),
             pltpu.SemaphoreType.DMA((3,)),

time: 60.4 us -> 60.3 us (level)
  the two profiles are of different devices: /device:TPU:39 before, /device:TPU:43 now
where the time goes in v7:
time: 60.3 us; the launch traced here: 60 us
  Pallas kernels  57.4 us (95%)
  local copies, waits for them, and re-layouts  1.99 us (3%)
  between operations  0.65 us (1%)
    pallas_call x1, Pallas kernels, local(): pl.pallas_call(functools.partial(kernel, rows, cols), out_shape=(jax.Shap...  57.4 us
    unnamed x4, local copies, waits for them, and re-layouts  1.99 us

profile of v7, /device:TPU:43, one launch (start us, length us, event | category | flops | bytes accessed | tf_op | source)
XLA Modules:
  0.0 60.0 jit_solution(9942534823445571124)
XLA Ops:
  0.6 57.4 %shard_map.77 = (f32[2,8,512]{2,1,0:T(8,128)}, f32[2,16,32]{2,1,0:T(8,128)}) custom-call(f32[256,128]{1,0:T(8,128)} %a_hbm.1, s32[32,32]{1,0:T(8,128)} %pattern_ref.1, s32[2,16]{1,0:T(2,128)} %listed_ref.1, f32[2,8,512]{2,1,0:T(8,128)} %panel_hbm.1, f32[512,512]{1,0:T(8,128)} %bitcast.3, f32[2,16,32]{2,1,0:T(8,128)} %bitcast.4), custom_call_target="tpu_custom_call" | custom-call | tf_op jit(solution)/shard_map/pallas_call | solution.py:517
  58.0 0.0 copy-start
  58.1 1.4 %copy.10 = f32[2,8,512]{2,1,0:T(8,128)} copy(f32[2,8,512]{2,1,0:T(8,128)} %get-tuple-element.8) | data formatting | bytes 65536
  59.4 0.0 copy-done
  59.4 0.6 %copy.11 = f32[2,32,16]{1,2,0:T(8,128)} copy(f32[2,32,16]{1,2,0:T(8,128)S(1)} %bitcast.5) | data formatting | bytes 8192
Async XLA Ops:
  58.0 1.4 %copy-start = (f32[2,16,32]{2,1,0:T(8,128)S(1)}, f32[2,16,32]{2,1,0:T(8,128)}, u32[]{:S(2)}) copy-start(f32[2,16,32]{2,1,0:T(8,128)} %get-tuple-element.5) | copy-start | bytes 12292

commit v8 on v7

--- a/solution.py
+++ b/solution.py
@@ -255,8 +255,7 @@
             pl.semaphore_signal(
                 ready, inc=1, device_id=(row, 2 * plane_at(-offset) + side), device_id_type=MESH
             )
-        for i in (2, 1):
-            anc_copy(i).start()
+        anc_copy(2).start()
 
     with jax.named_scope("early"):
         for h in range(2):
@@ -282,6 +281,7 @@
             extra_out[h] = extra[h * height : (h + 1) * height]
         extra_swap = chip_copy(extra_out.at[1 - core], extra_in, extra_sent, extra_got)
         extra_swap.start()
+        anc_copy(1).start()
         pl.semaphore_wait(ready, len(HOPS))
         for super_of in range(2):
             spread(0, super_of)
@@ -442,7 +442,7 @@
     with jax.named_scope("tiles"):
         pl.when(side == 1)(finish_upper)
 
-        for other in range(count):
+        for other in (2, 3, 4, 5, 6, 7, 0, 1, *range(8, count)):
             target = side * count + other
 
             def send():

time: 60.3 us -> 60.3 us (level)
  the two profiles are of different devices: /device:TPU:43 before, /device:TPU:1 now
where the time goes in v8:
time: 60.3 us; the launch traced here: 59.7 us
  Pallas kernels  57.1 us (95%)
  local copies, waits for them, and re-layouts  1.99 us (3%)
  between operations  0.65 us (1%)
    pallas_call x1, Pallas kernels, local(): pl.pallas_call(functools.partial(kernel, rows, cols), out_shape=(jax.Shap...  57.1 us
    unnamed x4, local copies, waits for them, and re-layouts  1.99 us

profile of v8, /device:TPU:1, one launch (start us, length us, event | category | flops | bytes accessed | tf_op | source)
XLA Modules:
  0.0 59.7 jit_solution(15542679510327688395)
XLA Ops:
  0.6 57.1 %shard_map.77 = (f32[2,8,512]{2,1,0:T(8,128)}, f32[2,16,32]{2,1,0:T(8,128)}) custom-call(f32[256,128]{1,0:T(8,128)} %a_hbm.1, s32[32,32]{1,0:T(8,128)} %pattern_ref.1, s32[2,16]{1,0:T(2,128)} %listed_ref.1, f32[2,8,512]{2,1,0:T(8,128)} %panel_hbm.1, f32[512,512]{1,0:T(8,128)} %bitcast.3, f32[2,16,32]{2,1,0:T(8,128)} %bitcast.4), custom_call_target="tpu_custom_call" | custom-call | tf_op jit(solution)/shard_map/pallas_call | solution.py:517
  57.7 0.0 copy-start
  57.7 1.4 %copy.10 = f32[2,8,512]{2,1,0:T(8,128)} copy(f32[2,8,512]{2,1,0:T(8,128)} %get-tuple-element.8) | data formatting | bytes 65536
  59.1 0.0 copy-done
  59.1 0.6 %copy.11 = f32[2,32,16]{1,2,0:T(8,128)} copy(f32[2,32,16]{1,2,0:T(8,128)S(1)} %bitcast.5) | data formatting | bytes 8192
Async XLA Ops:
  57.7 1.4 %copy-start = (f32[2,16,32]{2,1,0:T(8,128)S(1)}, f32[2,16,32]{2,1,0:T(8,128)}, u32[]{:S(2)}) copy-start(f32[2,16,32]{2,1,0:T(8,128)} %get-tuple-element.5) | copy-start | bytes 12292
